TPU v7x, 512 devices: a whole 4x4x16 slice. The times are simulated.
512 devices in a mesh: ctx: 128 (over x, z, core), mp: 4 (over y).
Axes of the slice: x: 4, y: 4, z: 16, core: 2. Of those that a mesh axis runs over, the one named last changes fastest.
Arguments:
- attn_query: bfloat16 [16384, 2048], P('ctx', 'mp'), may hold values from -160 to 160
- attn_key: bfloat16 [16384, 2048], P('ctx', 'mp'), may hold values from -8 to 8
- attn_value: bfloat16 [16384, 2048], P('ctx', 'mp'), may hold values from -6 to 6
- attn_cotangent: bfloat16 [16384, 2048], P('ctx', 'mp'), may hold values from -6 to 6
- hyena_query: bfloat16 [16384, 2048], P('ctx', 'mp'), may hold values from -300 to 300
- hyena_key: bfloat16 [16384, 2048], P('ctx', 'mp'), may hold values from -6 to 6
- hyena_value: bfloat16 [16384, 2048], P('ctx', 'mp'), may hold values from -6 to 6
- hyena_cotangent: bfloat16 [16384, 2048], P('ctx', 'mp'), may hold values from -6 to 6
- filter_taps: float32 [2048, 128], P('mp'), may hold values from -0.5 to 0.5
- norm_gain: float32 [2048], P('mp'), may hold values from 0.1 to 1.9
- segment_ids: int32 [16384], replicated, may hold values from 0 to 63, never falling along the last dimension, each value on 1 to 512 neighbouring positions
Outputs:
- attn_query_grad: bfloat16 [16384, 2048], P('ctx', 'mp')
- attn_key_grad: bfloat16 [16384, 2048], P('ctx', 'mp')
- attn_value_grad: bfloat16 [16384, 2048], P('ctx', 'mp')
- hyena_query_grad: bfloat16 [16384, 2048], P('ctx', 'mp')
- hyena_key_grad: bfloat16 [16384, 2048], P('ctx', 'mp')
- hyena_value_grad: bfloat16 [16384, 2048], P('ctx', 'mp')
- filter_grad: float32 [2048, 128], P('mp')
Inputs may be any that keep to these rules, and one draw needn't show every extreme that they name: `segment_ids`: documents are runs of equal ids, each at most 512 tokens long.
All inputs are finite; a program needn't handle non-finite values.
Results may differ from a plain program's by a relative error of at most 0.0085.
Values may be sent and summed in bfloat16 or wider, within the bound.
A program may use at most 64 MiB of HBM per device.

v0:
```python
import jax
import jax.numpy as jnp
from jax import lax
from jax.sharding import PartitionSpec as P

SPAN = 4
HEAD_DIM = 128
CHANNELS = 2048
TAPS = 128


def shifted(value, axis, steps):
    count = lax.axis_size(axis)
    leading, last = (max(0, -steps), min(count, count - steps))
    return lax.ppermute(value, axis, [(source, source + steps) for source in range(leading, last)])


def over_taps(step, init):

    def group(index, carry):
        for inner in range(8):
            carry = step(index * 8 + inner, carry)
        return carry

    return lax.fori_loop(0, TAPS // 8, group, init)


def pass_keys(block_pair, distance):
    return shifted(block_pair, "ctx", distance)


def pass_grads(block_terms, distance):
    return shifted(block_terms.astype(jnp.bfloat16), "ctx", distance).astype(block_terms.dtype)


def attend(query, keys, values, grad_out, allowed):
    scale = HEAD_DIM ** (-0.5)
    scores = jnp.einsum("qhd,khd->hqk", query, keys, preferred_element_type=jnp.float32) * scale
    scores = jnp.where(allowed[None], scores, -jnp.inf)
    peak = jnp.max(scores, axis=-1, keepdims=True)
    weights = jnp.exp(scores - peak)
    total = jnp.sum(weights, axis=-1, keepdims=True)
    weights = weights / total
    log_total = (peak + jnp.log(total))[:, :, 0].T
    rounded = weights.astype(jnp.bfloat16)
    output = jnp.einsum("hqk,khd->qhd", rounded, values, preferred_element_type=jnp.float32)
    offset = jnp.sum(grad_out.astype(jnp.float32) * output, axis=-1)
    grad_values = jnp.einsum("hqk,qhd->khd", rounded, grad_out, preferred_element_type=jnp.float32)
    grad_weights = jnp.einsum("qhd,khd->hqk", grad_out, values, preferred_element_type=jnp.float32)
    grad_scores = (weights * (grad_weights - offset.T[:, :, None])).astype(jnp.bfloat16)
    grad_query = (
        jnp.einsum("hqk,khd->qhd", grad_scores, keys, preferred_element_type=jnp.float32) * scale
    )
    grad_keys = (
        jnp.einsum("hqk,qhd->khd", grad_scores, query, preferred_element_type=jnp.float32) * scale
    )
    return (grad_query, grad_keys, grad_values, log_total, offset)


def body(
    attn_query,
    attn_key,
    attn_value,
    attn_cotangent,
    hyena_query,
    hyena_key,
    hyena_value,
    hyena_cotangent,
    filter_taps,
    norm_gain,
    segment_ids,
):
    rows, width = attn_query.shape
    heads = width // HEAD_DIM
    place = lax.axis_index("ctx")
    total = segment_ids.shape[0]
    start = place * rows
    pair = jnp.stack((attn_key, attn_value))
    blocks = [pair] + [pass_keys(pair, step) for step in range(1, SPAN + 1)]
    joined = jnp.concatenate(blocks, axis=1)
    key_count = (SPAN + 1) * rows
    key_all = joined[0].reshape(key_count, heads, HEAD_DIM)
    value_all = joined[1].reshape(key_count, heads, HEAD_DIM)
    offsets = jnp.arange(key_count, dtype=jnp.int32)
    key_pos = (place - offsets // rows) * rows + offsets % rows
    key_seg = jnp.take(segment_ids, jnp.clip(key_pos, 0, total - 1))
    query_pos = start + jnp.arange(rows, dtype=jnp.int32)
    query_seg = lax.dynamic_slice_in_dim(segment_ids, start, rows, 0)
    allowed = (
        (query_seg[:, None] == key_seg[None, :])
        & (key_pos[None, :] <= query_pos[:, None])
        & (key_pos[None, :] >= 0)
    )
    query_heads = attn_query.reshape(rows, heads, HEAD_DIM)
    grad_heads = attn_cotangent.reshape(rows, heads, HEAD_DIM)
    grad_query, grad_keys, grad_values, log_total, offset = attend(
        query_heads, key_all, value_all, grad_heads, allowed
    )
    key_terms = jnp.stack(
        (grad_keys.reshape(key_count, width), grad_values.reshape(key_count, width))
    ).reshape(2, SPAN + 1, rows, width)
    summed = key_terms[:, 0]
    for step in range(1, SPAN + 1):
        summed = summed + pass_grads(key_terms[:, step], -step)
    key_sum = summed[0]
    value_sum = summed[1]
    attn_query_grad = grad_query.reshape(rows, width).astype(jnp.bfloat16)
    attn_key_grad = key_sum.astype(jnp.bfloat16)
    attn_value_grad = value_sum.astype(jnp.bfloat16)
    chans = hyena_query.shape[1]
    rim_rows = TAPS - 1
    key_wide = hyena_key.astype(jnp.float32)
    value_wide = hyena_value.astype(jnp.float32)
    product = key_wide * value_wide
    rim = shifted(product[rows - rim_rows :].astype(jnp.bfloat16), "ctx", 1).astype(jnp.float32)
    extended = jnp.concatenate([rim, product])
    ext_seg = jnp.take(
        segment_ids,
        jnp.clip(start - rim_rows + jnp.arange(rows + rim_rows, dtype=jnp.int32), 0, total - 1),
    )
    own_seg = ext_seg[rim_rows:]

    def conv_step(tap, acc):
        piece = lax.dynamic_slice_in_dim(extended, rim_rows - tap, rows, 0)
        same = lax.dynamic_slice_in_dim(ext_seg, rim_rows - tap, rows, 0) == own_seg
        coeff = lax.dynamic_index_in_dim(filter_taps, tap, 1, keepdims=False)
        return acc + jnp.where(same[:, None], piece * coeff[None, :], 0.0)

    mixed = over_taps(conv_step, jnp.zeros((rows, chans), jnp.float32))
    query_wide = hyena_query.astype(jnp.float32)
    gated = query_wide * mixed
    weighted = norm_gain[None, :] * hyena_cotangent.astype(jnp.float32)
    squares, crossed = lax.psum(
        (jnp.sum(gated * gated, axis=-1), jnp.sum(weighted * gated, axis=-1)), "mp"
    )
    inverse = lax.rsqrt(squares / CHANNELS + 1e-06)
    gated_grad = inverse[:, None] * weighted - gated * (inverse**3 * (crossed / CHANNELS))[:, None]
    hyena_query_grad = (gated_grad * mixed).astype(jnp.bfloat16)
    signal = gated_grad * query_wide

    def filter_step(tap, acc):
        piece = lax.dynamic_slice_in_dim(extended, rim_rows - tap, rows, 0)
        same = lax.dynamic_slice_in_dim(ext_seg, rim_rows - tap, rows, 0) == own_seg
        column = jnp.sum(jnp.where(same[:, None], piece * signal, 0.0), axis=0)
        return lax.dynamic_update_slice_in_dim(acc, column[:, None], tap, 1)

    filter_terms = over_taps(filter_step, jnp.zeros((chans, TAPS), jnp.float32))
    filter_grad = lax.psum(filter_terms, "ctx") * total ** (-0.5)
    padded = jnp.concatenate(
        [
            jnp.zeros((rim_rows, chans), jnp.float32),
            signal,
            jnp.zeros((rim_rows, chans), jnp.float32),
        ]
    )
    pad_seg = jnp.take(
        segment_ids,
        jnp.clip(start - rim_rows + jnp.arange(rows + 2 * rim_rows, dtype=jnp.int32), 0, total - 1),
    )

    def spread_step(tap, acc):
        piece = lax.dynamic_slice_in_dim(padded, tap, rows + rim_rows, 0)
        same = lax.dynamic_slice_in_dim(pad_seg, tap, rows + rim_rows, 0) == ext_seg
        coeff = lax.dynamic_index_in_dim(filter_taps, tap, 1, keepdims=False)
        return acc + jnp.where(same[:, None], piece * coeff[None, :], 0.0)

    spread = over_taps(spread_step, jnp.zeros((rows + rim_rows, chans), jnp.float32))
    returned = shifted(spread[:rim_rows].astype(jnp.bfloat16), "ctx", -1).astype(jnp.float32)
    product_grad = spread[rim_rows:] + jnp.concatenate(
        [jnp.zeros((rows - rim_rows, chans), jnp.float32), returned]
    )
    hyena_key_grad = (product_grad * value_wide).astype(jnp.bfloat16)
    hyena_value_grad = (product_grad * key_wide).astype(jnp.bfloat16)
    return (
        attn_query_grad,
        attn_key_grad,
        attn_value_grad,
        hyena_query_grad,
        hyena_key_grad,
        hyena_value_grad,
        filter_grad,
    )


def solution(mesh):
    in_specs = (
        P("ctx", "mp"),
        P("ctx", "mp"),
        P("ctx", "mp"),
        P("ctx", "mp"),
        P("ctx", "mp"),
        P("ctx", "mp"),
        P("ctx", "mp"),
        P("ctx", "mp"),
        P("mp", None),
        P("mp"),
        P(),
    )
    out_specs = (
        P("ctx", "mp"),
        P("ctx", "mp"),
        P("ctx", "mp"),
        P("ctx", "mp"),
        P("ctx", "mp"),
        P("ctx", "mp"),
        P("mp", None),
    )
    return jax.shard_map(body, mesh=mesh, in_specs=in_specs, out_specs=out_specs, check_vma=False)
```

profile of v0, /device:TPU:1, one launch (start us, length us, event | category | flops | bytes accessed | tf_op | source)
XLA Modules:
  0.0 504.2 jit_solution(678497068434085569)
XLA Ops:
  7.3 1.2 copy.29
  8.4 1.0 copy.28
  9.5 0.8 pad_maximum_fusion.2
  10.3 4.9 collective-permute-start
  15.2 4.3 collective-permute-start.1
  19.5 2.9 collective-permute-start.2
  22.3 6.1 %collective-permute-start.3 = (bf16[2,128,512]{1,2,0:T(8,128)(2,1)S(1)}, bf16[2,128,512]{1,2,0:T(8,128)(2,1)S(1)}, u32[]{:S(2)}, u32[]{:S(2)}) collective-permute-start(bf16[2,128,512]{1,2,0:T(8,128)(2,1)S(1)} %get-tuple-element.743), channel_id=1, source_target_pairs={{0,16},{4,20},{8,24},{12,28},{16,32},{20,36},{24,40},{28,44},{32,4... | collective-permute-start | bytes 786440 | tf_op jit(solution)/shard_map/ppermute | solution.py:15
  28.5 4.1 collective-permute-start.8
  33.6 3.9 gather_fusion
  37.5 1.7 gather_fusion.1
  39.5 2.5 gather_fusion.2
  42.0 1.0 and_and_fusion
  43.1 11.2 %while.50 = (s32[]{:T(128)}, f32[128,512]{1,0:T(8,128)S(1)}, s32[255]{0:T(256)S(1)}, s32[128]{0:T(128)S(1)}, f32[255,512]{1,0:T(8,128)S(1)}, /*index=5*/f32[512,...) while((s32[]{:T(128)}, f32[128,512]{1,0:T(8,128)S(1)}, ...), condition=%wide.region_4.5_spmd.clone, body=%wide.region_3.4_spmd.clone.sunk | while | flops 1639491 | bytes 2678319 | solution.py:25
  54.5 8.7 %all-reduce.1 = (f32[128]{0:T(128)S(1)}, f32[128]{0:T(128)S(1)}) all-reduce(f32[128]{0:T(128)S(1)} %get-tuple-element.652, f32[128]{0:T(128)S(1)} %get-tuple-element.651), channel_id=1, replica_groups=mesh['ctx'=128,'mp'=4] {'mp'}, use_global_device_ids=true, to_apply=%region_8.9 | all-reduce | flops 256 | bytes 2048 | tf_op jit(solution)/shard_map/psum | solution.py:133
  63.3 0.8 convert_multiply_fusion.3
  64.2 53.2 %while.51 = (s32[]{:T(128)}, f32[255,512]{1,0:T(8,128)S(1)}, s32[382]{0:T(512)S(1)}, s32[255]{0:T(256)S(1)}, f32[382,512]{1,0:T(8,128)S(1)}, /*index=5*/f32[512,...) while((s32[]{:T(128)}, f32[255,512]{1,0:T(8,128)S(1)}, ...), condition=%wide.region_10.11_spmd.clone, body=%wide.region_9.10_spmd.clone.sunk | while | flops 3266091 | bytes 5285763 | solution.py:25
  65.6 1.9 fusion.93
  68.9 1.9 fusion.93
  72.2 1.9 fusion.93
  75.5 1.9 fusion.93
  78.9 1.9 fusion.93
  82.2 1.9 fusion.93
  85.5 1.9 fusion.93
  88.8 1.9 fusion.93
  92.2 1.9 fusion.93
  95.5 1.9 fusion.93
  98.8 1.9 fusion.93
  102.1 1.9 fusion.93
  105.5 1.9 fusion.93
  108.8 1.9 fusion.93
  112.1 1.9 fusion.93
  115.4 1.9 fusion.93
  117.4 2.4 collective-permute-start.9
  119.9 31.6 %while.49 = (s32[]{:T(128)}, f32[512,128]{0,1:T(8,128)S(1)}, s32[255]{0:T(256)S(1)}, s32[128]{0:T(128)}, f32[255,512]{1,0:T(8,128)S(1)}, /*index=5*/f32[128,512]...) while((s32[]{:T(128)}, f32[512,128]{0,1:T(8,128)S(1)}, ...), condition=%wide.region_20.21_spmd, body=%wide.region_11.20_spmd.sunk | while | flops 1569858 | bytes 2416165 | solution.py:25
  120.0 0.8 dynamic-slice_compare_fusion.27
  121.9 0.8 dynamic-slice_compare_fusion.27
  125.9 0.8 dynamic-slice_compare_fusion.27
  131.8 0.8 dynamic-slice_compare_fusion.27
  141.7 0.8 dynamic-slice_compare_fusion.27
  143.6 0.8 dynamic-slice_compare_fusion.27
  151.5 0.8 copy.47
  152.3 0.8 fusion.32
  153.1 1.7 constant_dynamic-update-slice_fusion.3
  154.9 1.7 constant_dynamic-update-slice_fusion.2
  158.1 1.4 fusion.72
  160.5 1.9 convolution_bitcast_fusion
  162.4 0.9 fusion.25
  163.2 1.2 fusion.22
  164.5 1.4 fusion.16
  165.9 0.8 copy.38
  166.7 1.6 stack.19
  168.4 1.5 constant_dynamic-update-slice_fusion.6
  170.1 1.9 copy.40
  172.0 2.7 stack.20
  174.7 1.4 constant_dynamic-update-slice_fusion.5
  176.3 1.0 slice_bitcast_fusion.4
  177.3 1.3 collective-permute-start.7
  178.6 1.3 collective-permute-start.6
  179.9 1.3 collective-permute-start.5
  181.2 1.9 collective-permute-start.4
  183.2 308.3 %all-reduce.4.cloned.1.call-done = f32[512,128]{1,0:T(8,128)} async-done(((f32[512,128]{1,0:T(8,128)}), f32[512,128]{1,0:T(8,128)}) %all-reduce.4.cloned.1.call-update) | async-done | bytes 262160 | tf_op jit(solution)/shard_map/psum | solution.py:148
  491.4 1.7 broadcast_multiply_fusion
  493.1 1.4 fusion.24
  495.3 1.4 fusion.31
  (304 shorter events, 59.7 us)
Async XLA Ops:
  7.2 152.4 %copy-start = (bf16[128,512]{1,0:T(8,128)(2,1)S(1)}, bf16[128,512]{1,0:T(8,128)(2,1)}, u32[]{:S(2)}) copy-start(bf16[128,512]{1,0:T(8,128)(2,1)} %param.17) | copy-start | bytes 393220
  7.2 21.3 %copy-start.3 = (bf16[128,512]{1,0:T(8,128)(2,1)S(1)}, bf16[128,512]{1,0:T(8,128)(2,1)}, u32[]{:S(2)}) copy-start(bf16[128,512]{1,0:T(8,128)(2,1)} %param.23) | copy-start | bytes 393220
  7.2 21.3 %copy-start.4 = (bf16[128,512]{1,0:T(8,128)(2,1)S(1)}, bf16[128,512]{1,0:T(8,128)(2,1)}, u32[]{:S(2)}) copy-start(bf16[128,512]{1,0:T(8,128)(2,1)} %param.22) | copy-start | bytes 393220
  7.2 25.6 %copy-start.8 = (bf16[128,512]{1,0:T(8,128)(2,1)S(1)}, bf16[128,512]{1,0:T(8,128)(2,1)}, u32[]{:S(2)}) copy-start(bf16[128,512]{1,0:T(8,128)(2,1)} %param.20) | copy-start | bytes 393220
  7.2 26.3 %copy-start.1 = (s32[16384]{0:T(1024)S(1)}, s32[16384]{0:T(1024)}, u32[]{:S(2)}) copy-start(s32[16384]{0:T(1024)} %param.27) | copy-start | bytes 196612
  7.2 484.2 %all-reduce.4.cloned.1.call-start = ((), (), s32[]{:S(2)}) async-start(), calls=%async_computation | async-start | bytes 524288 | tf_op jit(solution)/shard_map/psum | solution.py:148
  10.3 142.9 %collective-permute-start = (bf16[2,128,512]{1,2,0:T(8,128)(2,1)S(1)}, bf16[2,128,512]{1,2,0:T(8,128)(2,1)}, u32[]{:S(2)}, u32[]{:S(2)}) collective-permute-start(bf16[2,128,512]{1,2,0:T(8,128)(2,1)S(1)} %get-tuple-element.743), channel_id=1, source_target_pairs={{0,4},{4,8},{8,12},{12,16},{16,20},{20,24},{24,28},{28,32},{32,36}... | collective-permute-start | bytes 786440 | tf_op jit(solution)/shard_map/ppermute | solution.py:15
  15.2 139.7 %collective-permute-start.1 = (bf16[2,128,512]{1,2,0:T(8,128)(2,1)S(1)}, bf16[2,128,512]{1,2,0:T(8,128)(2,1)}, u32[]{:S(2)}, u32[]{:S(2)}) collective-permute-start(bf16[2,128,512]{1,2,0:T(8,128)(2,1)S(1)} %get-tuple-element.743), channel_id=1, source_target_pairs={{0,8},{4,12},{8,16},{12,20},{16,24},{20,28},{24,32},{28,36},{32,40... | collective-permute-start | bytes 786440 | tf_op jit(solution)/shard_map/ppermute | solution.py:15
  19.5 137.1 %collective-permute-start.2 = (bf16[2,128,512]{1,2,0:T(8,128)(2,1)S(1)}, bf16[2,128,512]{1,2,0:T(8,128)(2,1)S(1)}, u32[]{:S(2)}, u32[]{:S(2)}) collective-permute-start(bf16[2,128,512]{1,2,0:T(8,128)(2,1)S(1)} %get-tuple-element.743), channel_id=1, source_target_pairs={{0,12},{4,16},{8,20},{12,24},{16,28},{20,32},{24,36},{28,40},{32,4... | collective-permute-start | bytes 786440 | tf_op jit(solution)/shard_map/ppermute | solution.py:15
  22.3 135.1 %collective-permute-start.3 = (bf16[2,128,512]{1,2,0:T(8,128)(2,1)S(1)}, bf16[2,128,512]{1,2,0:T(8,128)(2,1)S(1)}, u32[]{:S(2)}, u32[]{:S(2)}) collective-permute-start(bf16[2,128,512]{1,2,0:T(8,128)(2,1)S(1)} %get-tuple-element.743), channel_id=1, source_target_pairs={{0,16},{4,20},{8,24},{12,28},{16,32},{20,36},{24,40},{28,44},{32,4... | collective-permute-start | bytes 786440 | tf_op jit(solution)/shard_map/ppermute | solution.py:15
  28.5 14.5 %collective-permute-start.8 = (bf16[127,512]{1,0:T(8,128)(2,1)S(1)}, bf16[127,512]{1,0:T(8,128)(2,1)S(1)}, u32[]{:S(2)}, u32[]{:S(2)}) collective-permute-start(bf16[127,512]{1,0:T(8,128)(2,1)S(1)} %slice.102), channel_id=1, source_target_pairs={{0,4},{4,8},{8,12},{12,16},{16,20},{20,24},{24,28},{28,32},{32,36}... | collective-permute-start | bytes 390152 | tf_op jit(solution)/shard_map/ppermute | solution.py:15
  33.6 5.7 %copy-start.7 = (f32[512,128]{1,0:T(8,128)S(1)}, f32[512,128]{1,0:T(8,128)}, u32[]{:S(2)}) copy-start(f32[512,128]{1,0:T(8,128)} %param.25) | copy-start | bytes 786436
  43.1 11.3 %copy-start.5 = (bf16[128,512]{1,0:T(8,128)(2,1)S(1)}, bf16[128,512]{1,0:T(8,128)(2,1)}, u32[]{:S(2)}) copy-start(bf16[128,512]{1,0:T(8,128)(2,1)} %param.21) | copy-start | bytes 393220
  43.1 11.3 %copy-start.6 = (bf16[128,512]{1,0:T(8,128)(2,1)S(1)}, bf16[128,512]{1,0:T(8,128)(2,1)}, u32[]{:S(2)}) copy-start(bf16[128,512]{1,0:T(8,128)(2,1)} %param.24) | copy-start | bytes 393220
  43.1 11.3 %copy-start.12 = (f32[512]{0:T(512)S(1)}, f32[512]{0:T(512)}, u32[]{:S(2)}) copy-start(f32[512]{0:T(512)} %param.26) | copy-start | bytes 6148
  54.4 9.7 %copy-start.11 = (s32[128]{0:T(128)}, s32[128]{0:T(128)S(1)}, u32[]{:S(2)}) copy-start(s32[128]{0:T(128)S(1)} %get-tuple-element.1221) | copy-start | bytes 1540
  117.4 34.9 %collective-permute-start.9 = (bf16[127,512]{1,0:T(8,128)(2,1)S(1)}, bf16[127,512]{1,0:T(8,128)(2,1)S(1)}, u32[]{:S(2)}, u32[]{:S(2)}) collective-permute-start(bf16[127,512]{1,0:T(8,128)(2,1)S(1)} %slice.101), channel_id=1, source_target_pairs={{4,0},{8,4},{12,8},{16,12},{20,16},{24,20},{28,24},{32,28},{36,32}... | collective-permute-start | bytes 390152 | tf_op jit(solution)/shard_map/ppermute | solution.py:15
  158.1 1.4 copy-start.10
  159.6 0.9 copy-start.9
  168.4 1.7 copy-start.2
  177.3 317.9 %collective-permute-start.7 = (bf16[2,128,512]{2,1,0:T(8,128)(2,1)}, bf16[2,128,512]{2,1,0:T(8,128)(2,1)}, u32[]{:S(2)}, u32[]{:S(2)}) collective-permute-start(bf16[2,128,512]{2,1,0:T(8,128)(2,1)} %get-tuple-element.733), channel_id=1, source_target_pairs={{16,0},{20,4},{24,8},{28,12},{32,16},{36,20},{40,24},{44,28},{48,3... | collective-permute-start | bytes 786440 | tf_op jit(solution)/shard_map/ppermute | solution.py:15
  178.6 316.7 %collective-permute-start.6 = (bf16[2,128,512]{2,1,0:T(8,128)(2,1)}, bf16[2,128,512]{2,1,0:T(8,128)(2,1)}, u32[]{:S(2)}, u32[]{:S(2)}) collective-permute-start(bf16[2,128,512]{2,1,0:T(8,128)(2,1)} %get-tuple-element.734), channel_id=1, source_target_pairs={{12,0},{16,4},{20,8},{24,12},{28,16},{32,20},{36,24},{40,28},{44,3... | collective-permute-start | bytes 786440 | tf_op jit(solution)/shard_map/ppermute | solution.py:15
  179.9 315.4 %collective-permute-start.5 = (bf16[2,128,512]{2,1,0:T(8,128)(2,1)}, bf16[2,128,512]{2,1,0:T(8,128)(2,1)}, u32[]{:S(2)}, u32[]{:S(2)}) collective-permute-start(bf16[2,128,512]{2,1,0:T(8,128)(2,1)} %get-tuple-element.732), channel_id=1, source_target_pairs={{8,0},{12,4},{16,8},{20,12},{24,16},{28,20},{32,24},{36,28},{40,32... | collective-permute-start | bytes 786440 | tf_op jit(solution)/shard_map/ppermute | solution.py:15
  181.2 314.1 %collective-permute-start.4 = (bf16[2,128,512]{2,1,0:T(8,128)(2,1)}, bf16[2,128,512]{2,1,0:T(8,128)(2,1)}, u32[]{:S(2)}, u32[]{:S(2)}) collective-permute-start(bf16[2,128,512]{2,1,0:T(8,128)(2,1)} %get-tuple-element.731), channel_id=1, source_target_pairs={{4,0},{8,4},{12,8},{16,12},{20,16},{24,20},{28,24},{32,28},{36,32}... | collective-permute-start | bytes 786440 | tf_op jit(solution)/shard_map/ppermute | solution.py:15
Sparse Core Ops, SparseCore 0:
  152.5 338.9 all-reduce.3
where the time goes:
time: 506 us; the launch traced here: 504 us
  waiting for transfers between devices  308 us (61%)
  other arithmetic  77.7 us (15%)
  local copies, waits for them, and re-layouts  50.2 us (10%)
  starting transfers between devices  30.5 us (6%)
  between operations  14.5 us (3%)
  blocking collectives  8.72 us (2%)
  matrix products  7.46 us (1%)
  loops' own time  6.84 us (1%)
    psum x1, waiting for transfers between devices, body(): filter_grad = lax.psum(filter_terms, 'ctx') * total ** (-0.5)  308 us
    add x16, other arithmetic, spread_step(): return acc + jnp.where(same[:, None], piece * coeff[None, :], 0.0)  30.7 us
    ppermute x10, starting transfers between devices, shifted(): lax.ppermute(value, axis, [(source, source + steps) for source in range(l...  30.5 us
    eq x16, other arithmetic, filter_step(): same = lax.dynamic_slice_in_dim(ext_seg, rim_rows - tap, rows, 0) == own_seg  12.5 us
    eq x16, other arithmetic, spread_step(): same = lax.dynamic_slice_in_dim(pad_seg, tap, rows + rim_rows, 0) == ext_seg  10.9 us
    dynamic_slice x16, local copies, waits for them, and re-layouts, spread_step(): coeff = lax.dynamic_index_in_dim(filter_taps, tap, 1, keepdims=False)  10.1 us
  transfers between devices with their start and end apart: 11, of which 1 were waited for; matrix products, arithmetic and copies ran while one was open for 26% of the time, Pallas kernels for 0%

commit v1 on v0

v1 whole, which is shorter than its diff:
```python
import jax
import jax.numpy as jnp
from jax import lax
from jax.experimental import pallas as pl
from jax.experimental.pallas import tpu as pltpu
from jax.sharding import PartitionSpec as P

SPAN = 4
HEAD_DIM = 128
TAPS = 128
ROWS = 128
LINE = 16
GROUP = 8
LANES = 128
F32 = jnp.float32
BF16 = jnp.bfloat16
FAR = -1e30
MESH = pl.DeviceIdType.MESH


def contract(left, right, left_dim, right_dim):
    return lax.dot_general(
        left, right, (((left_dim,), (right_dim,)), ((), ())), preferred_element_type=F32
    )


def make_kernel(n, m, width, line):
    heads = width // HEAD_DIM
    columns = width // LANES
    channels = width * m
    slabs = n // line
    slab_taps = TAPS // slabs
    row_taps = slab_taps // line
    keys = (SPAN + 1) * ROWS
    scale = HEAD_DIM ** (-0.5)

    def lanes(index):
        return pl.ds(pl.multiple_of(index * LANES, LANES), LANES)

    def kernel(
        aq, ak, av, ao, hq, hk, hv, ho, taps, gain, seg,
        daq, dak, dav, dhq, dhk, dhv, dfilter,
        segrows, segcols, bias, taps_t, ext, halo_out, halo_in, shifts,
        mixed, gated, weighted, squares, crossed, sums, sums_in,
        sig, sig_out, sig_in, back, ft, fa_out, fa_in, fb_out, fb_in, fc, fd,
        kv, grads, gs_out, gs_in, g2_out, g2_in, g1_out, g1_in,
        one_send, one_recv, mp_send, mp_recv, kv_send, kv_recv,
        g_send, g_recv, slab_send, slab_recv, line_send, line_recv,
    ):
        i = lax.axis_index("ctx")
        j = lax.axis_index("mp")
        core = lax.rem(i, 2)
        chip = i // 2
        z = lax.rem(chip, line)
        x = chip // line
        slab = x * 2 + core
        after, before = lax.rem(i + 1, n), lax.rem(i + n - 1, n)
        ahead, behind = lax.rem(i + 2, n), lax.rem(i + n - 2, n)
        sibling = i + 1 - 2 * core

        def copy(src, dst, send, recv, device):
            return pltpu.make_async_remote_copy(
                src_ref=src, dst_ref=dst, send_sem=send, recv_sem=recv,
                device_id=device, device_id_type=MESH,
            )

        def slab_peer(step):
            other = lax.rem(slab + step, slabs)
            return other, ((other // 2) * line + z) * 2 + lax.rem(other, 2)

        def line_peer(step):
            other = lax.rem(z + step, line)
            return other, (x * line + other) * 2 + core

        barrier = pltpu.get_barrier_semaphore()

        def greet(device):
            pl.semaphore_signal(barrier, inc=1, device_id=device, device_id_type=MESH)

        for device in (after, before, ahead, behind, sibling):
            greet({"ctx": device})
        for step in range(1, m):
            greet({"mp": lax.rem(j + step, m)})

        @pl.loop(1, slabs)
        def _(step):
            greet({"ctx": slab_peer(step)[1]})

        @pl.loop(1, line)
        def _(step):
            greet({"ctx": line_peer(step)[1]})

        product = hk[...].astype(F32) * hv[...].astype(F32)
        ext[ROWS:, :] = product
        halo_out[...] = product.astype(BF16)
        for head in range(heads):
            part = slice(head * HEAD_DIM, (head + 1) * HEAD_DIM)
            kv[head, 0, 0] = ak[:, part]
            kv[head, 0, 1] = av[:, part]

        pl.semaphore_wait(barrier, 5 + (m - 1) + (slabs - 1) + (line - 1))

        halo_copy = copy(halo_out, halo_in, one_send.at[0], one_recv.at[0], {"ctx": after})
        halo_copy.start()

        def own_copy(head):
            return copy(
                kv.at[head, 0], kv.at[head, 2], kv_send.at[head, 0], kv_recv.at[head, 0],
                {"ctx": ahead},
            )

        def pass_copy(head):
            return copy(
                kv.at[head, 2], kv.at[head, 4], kv_send.at[head, 1], kv_recv.at[head, 1],
                {"ctx": ahead},
            )

        def near_copy(head):
            return copy(
                kv.at[head, 2 * core], kv.at[head, 1], kv_send.at[head, 2], kv_recv.at[head, 2],
                {"ctx": sibling},
            )

        def far_copy(head):
            return copy(
                kv.at[head, 2 * core + 2], kv.at[head, 3], kv_send.at[head, 3],
                kv_recv.at[head, 3], {"ctx": sibling},
            )

        @pl.loop(0, heads)
        def _(head):
            own_copy(head).start()

        def first_service(head):
            own_copy(head).wait_recv()
            pass_copy(head).start()
            near_copy(head).start()

        def second_service(head):
            pass_copy(head).wait_recv()
            far_copy(head).start()

        segrows[...] = jnp.zeros_like(segrows)
        for row in range(SPAN + 2):
            block = i - SPAN + row
            inside = (block >= 0) & (block < n)
            held = seg[pl.ds(jnp.clip(block, 0, n - 1), 1), :]
            segrows[row : row + 1, :] = jnp.where(inside, held, -1 if row < SPAN else -2).astype(F32)
        turned = segrows[...].T
        for place in range(3):
            row = SPAN - 1 + place
            segcols[place * ROWS : (place + 1) * ROWS, :] = jnp.broadcast_to(
                turned[:, row : row + 1], (ROWS, LANES)
            )
        query_seg = segrows[SPAN : SPAN + 1, :]
        key_at = lax.broadcasted_iota(jnp.int32, (ROWS, ROWS), 0)
        query_at = lax.broadcasted_iota(jnp.int32, (ROWS, ROWS), 1)
        for back_by in range(SPAN + 1):
            row = SPAN - back_by
            allowed = turned[:, row : row + 1] == query_seg
            if back_by == 0:
                allowed = allowed & (key_at <= query_at)
            bias[back_by * ROWS : (back_by + 1) * ROWS, :] = jnp.where(allowed, 0.0, FAR)
        taps_t[...] = taps[...].T

        halo_copy.wait_recv()
        ext[:ROWS, :] = halo_in[...].astype(F32)

        @pl.loop(0, columns)
        def _(column):
            part = lanes(column)
            for r in range(GROUP):
                same = segcols[GROUP - r : 2 * ROWS - r, :] == segcols[GROUP : 2 * ROWS, :]
                shifts[r, GROUP : 2 * ROWS, part] = jnp.where(
                    same, ext[GROUP - r : 2 * ROWS - r, part], 0.0
                )

        def convolve(column):
            part = lanes(column)
            own = segcols[ROWS : 2 * ROWS, :]

            def step(a, total):
                base = pl.multiple_of(ROWS - GROUP * a, GROUP)
                coeff = taps_t[pl.ds(pl.multiple_of(GROUP * a, GROUP), GROUP), part]
                term = coeff[0:1] * shifts[0, pl.ds(base, ROWS), part]
                for r in range(1, GROUP):
                    term = term + coeff[r : r + 1] * shifts[r, pl.ds(base, ROWS), part]
                same = segcols[pl.ds(base, ROWS), :] == own
                return total + jnp.where(same, term, 0.0)

            found = lax.fori_loop(0, TAPS // GROUP, step, jnp.zeros((ROWS, LANES), F32))
            mixed[:, part] = found
            gate = hq[:, part].astype(F32) * found
            heavy = gain[:, part] * ho[:, part].astype(F32)
            gated[:, part] = gate
            weighted[:, part] = heavy
            squares[...] += gate * gate
            crossed[...] += heavy * gate

        squares[...] = jnp.zeros_like(squares)
        crossed[...] = jnp.zeros_like(crossed)

        @pl.loop(0, columns)
        def _(column):
            convolve(column)
            first_service(column)

        square_sum = jnp.sum(squares[...], axis=1, keepdims=True)
        cross_sum = jnp.sum(crossed[...], axis=1, keepdims=True)
        lane_at = lax.broadcasted_iota(jnp.int32, (ROWS, LANES), 1)
        squares[...] = jnp.where(lane_at == 0, square_sum, jnp.where(lane_at == 1, cross_sum, 0.0))
        sums[...] = squares[...].T[0:8]

        def sum_copy(step):
            return copy(
                sums, sums_in.at[step - 1], mp_send.at[step - 1], mp_recv.at[step - 1],
                {"mp": lax.rem(j + step, m)},
            )

        for step in range(1, m):
            sum_copy(step).start()
        for step in range(1, m):
            sum_copy(step).wait_recv()
        whole = sums[...]
        for step in range(1, m):
            whole = whole + sums_in[step - 1]
        inverse = lax.rsqrt(whole[0:1] / channels + 1e-06)
        factor = inverse * inverse * inverse * (whole[1:2] / channels)
        squares[0:1, :] = inverse
        squares[1:2, :] = factor
        upright = squares[...].T
        squares[...] = jnp.broadcast_to(upright[:, 0:1], (ROWS, LANES))
        crossed[...] = jnp.broadcast_to(upright[:, 1:2], (ROWS, LANES))

        @pl.loop(0, columns)
        def _(column):
            part = lanes(column)
            slope = squares[...] * weighted[:, part] - gated[:, part] * crossed[...]
            dhq[:, part] = (slope * mixed[:, part]).astype(BF16)
            signal = slope * hq[:, part].astype(F32)
            sig[:ROWS, part] = signal
            sig_out[:, part] = signal.astype(BF16)

        sig_copy = copy(sig_out, sig_in, one_send.at[1], one_recv.at[1], {"ctx": before})
        sig_copy.start()

        def correlate(column):
            part = lanes(column)
            own = segcols[ROWS : 2 * ROWS, :]
            signal = sig[:ROWS, part]

            @pl.loop(0, TAPS // GROUP)
            def _(a):
                base = pl.multiple_of(ROWS - GROUP * a, GROUP)
                same = segcols[pl.ds(base, ROWS), :] == own
                masked = jnp.where(same, signal, 0.0)
                found = [
                    jnp.sum(masked * shifts[r, pl.ds(base, ROWS), part], axis=0, keepdims=True)
                    for r in range(GROUP)
                ]
                ft[pl.ds(pl.multiple_of(GROUP * a, GROUP), GROUP), part] = jnp.concatenate(found)

        @pl.loop(0, columns)
        def _(column):
            correlate(column)
            second_service(column)

        for place in range(slabs):
            fa_out[place] = ft[place * slab_taps : (place + 1) * slab_taps, :].astype(BF16)

        def fa_copy(step):
            other, device = slab_peer(step)
            return copy(
                fa_out.at[other], fa_in.at[step - 1], slab_send.at[0, step - 1],
                slab_recv.at[0, step - 1], {"ctx": device},
            )

        def fb_copy(step):
            other, device = line_peer(step)
            return copy(
                fb_out.at[other], fb_in.at[step - 1], line_send.at[0, step - 1],
                line_recv.at[0, step - 1], {"ctx": device},
            )

        def fc_copy(step):
            _, device = line_peer(step)
            return copy(
                fc.at[z], fc.at[z], line_send.at[1, step - 1], line_recv.at[1, step - 1],
                {"ctx": device},
            )

        def fd_copy(step):
            _, device = slab_peer(step)
            return copy(
                fd.at[slab], fd.at[slab], slab_send.at[1, step - 1], slab_recv.at[1, step - 1],
                {"ctx": device},
            )

        def start_all(make, count):
            @pl.loop(1, count)
            def _(step):
                make(step).start()

        def recv_all(make, count):
            @pl.loop(1, count)
            def _(step):
                make(step).wait_recv()

        def send_all(make, count):
            @pl.loop(1, count)
            def _(step):
                make(step).wait_send()

        start_all(fa_copy, slabs)

        def attend(head):
            part = lanes(head)
            near_copy(head).wait_recv()
            far_copy(head).wait_recv()
            query, cot = aq[:, part], ao[:, part]
            key_all = kv[head, :, 0].reshape(keys, HEAD_DIM)
            value_all = kv[head, :, 1].reshape(keys, HEAD_DIM)
            scores = contract(key_all, query, 1, 1) * scale + bias[...]
            peak = jnp.max(scores, axis=0, keepdims=True)
            powers = jnp.exp(scores - peak)
            probs = powers * (1.0 / jnp.sum(powers, axis=0, keepdims=True))
            low = probs.astype(BF16)
            slope = contract(value_all, cot, 1, 1)
            offset = jnp.sum(low.astype(F32) * slope, axis=0, keepdims=True)
            score_grad = (probs * (slope - offset)).astype(BF16)
            daq[:, part] = (contract(score_grad, key_all, 0, 0) * scale).astype(BF16)
            grads[head, 0] = contract(score_grad, query, 1, 0) * scale
            grads[head, 1] = contract(low, cot, 1, 0)
            for place in range(2):
                rows = slice((2 * place + 1) * ROWS, (2 * place + 2) * ROWS)
                gs_out[head, place] = grads[head, :, rows].astype(BF16)
            gs_copy(head).start()

        def gs_copy(head):
            return copy(
                gs_out.at[head], gs_in.at[head], g_send.at[head, 0], g_recv.at[head, 0],
                {"ctx": sibling},
            )

        def g2_copy(head):
            return copy(
                g2_out.at[head], g2_in.at[head], g_send.at[head, 1], g_recv.at[head, 1],
                {"ctx": behind},
            )

        def g1_copy(head):
            return copy(
                g1_out.at[head], g1_in.at[head], g_send.at[head, 2], g_recv.at[head, 2],
                {"ctx": behind},
            )

        first_core = core == 0

        def return_two(head):
            gs_copy(head).wait_recv()
            mine = grads[head, :, 4 * ROWS : 5 * ROWS]
            theirs = gs_in[head, 1].astype(F32)
            g2_out[head] = (mine + jnp.where(first_core, 0.0, theirs)).astype(BF16)
            g2_copy(head).start()

        def return_one(head):
            g2_copy(head).wait_recv()
            mine = grads[head, :, 2 * ROWS : 3 * ROWS]
            theirs = jnp.where(first_core, gs_in[head, 1].astype(F32), gs_in[head, 0].astype(F32))
            g1_out[head] = (mine + theirs + g2_in[head].astype(F32)).astype(BF16)
            g1_copy(head).start()

        def return_own(head):
            part = lanes(head)
            g1_copy(head).wait_recv()
            mine = grads[head, :, 0:ROWS]
            theirs = jnp.where(first_core, gs_in[head, 0].astype(F32), 0.0)
            done = mine + theirs + g1_in[head].astype(F32)
            dak[:, part] = done[0].astype(BF16)
            dav[:, part] = done[1].astype(BF16)

        half = heads // 2

        @pl.loop(0, half)
        def _(head):
            attend(head)

        recv_all(fa_copy, slabs)
        slab_sum = ft[pl.ds(pl.multiple_of(slab * slab_taps, slab_taps), slab_taps), :]
        for step in range(1, slabs):
            slab_sum = slab_sum + fa_in[step - 1].astype(F32)
        for place in range(line):
            fb_out[place] = slab_sum[place * row_taps : (place + 1) * row_taps]
        start_all(fb_copy, line)

        @pl.loop(half, heads)
        def _(head):
            attend(head)
            return_two(head - half)

        recv_all(fb_copy, line)
        row_sum = fb_out[z]
        for step in range(1, line):
            row_sum = row_sum + fb_in[step - 1]
        fc[z] = row_sum * (n * ROWS) ** (-0.5)
        start_all(fc_copy, line)

        @pl.loop(half, heads)
        def _(head):
            return_two(head)

        sig_copy.wait_recv()
        sig[ROWS:, :] = sig_in[...].astype(F32)
        reach = 2 * ROWS - GROUP

        def spread(column):
            part = lanes(column)
            own = segcols[ROWS : 2 * ROWS, :]
            for r in range(GROUP):
                same = segcols[ROWS + r : ROWS + r + reach, :] == segcols[ROWS : ROWS + reach, :]
                back[r] = jnp.where(same, sig[r : r + reach, part], 0.0)

            def step(a, total):
                base = pl.multiple_of(GROUP * a, GROUP)
                coeff = taps_t[pl.ds(base, GROUP), part]
                term = coeff[0:1] * back[0, pl.ds(base, ROWS), :]
                for r in range(1, GROUP):
                    term = term + coeff[r : r + 1] * back[r, pl.ds(base, ROWS), :]
                same = segcols[pl.ds(pl.multiple_of(ROWS + base, GROUP), ROWS), :] == own
                return total + jnp.where(same, term, 0.0)

            found = lax.fori_loop(0, TAPS // GROUP, step, jnp.zeros((ROWS, LANES), F32))
            dhk[:, part] = (found * hv[:, part].astype(F32)).astype(BF16)
            dhv[:, part] = (found * hk[:, part].astype(F32)).astype(BF16)

        @pl.loop(0, columns)
        def _(column):
            spread(column)
            return_one(column)

        recv_all(fc_copy, line)
        fd[slab] = jnp.concatenate([fc[place] for place in range(line)]).astype(BF16)
        start_all(fd_copy, slabs)

        @pl.loop(0, heads)
        def _(head):
            return_own(head)

        recv_all(fd_copy, slabs)
        dfilter[...] = fd[...].reshape(TAPS, width).astype(F32).T

        halo_copy.wait_send()
        sig_copy.wait_send()
        for step in range(1, m):
            sum_copy(step).wait_send()

        @pl.loop(0, heads)
        def _(head):
            for made in (own_copy, pass_copy, near_copy, far_copy, gs_copy, g2_copy, g1_copy):
                made(head).wait_send()

        send_all(fa_copy, slabs)
        send_all(fb_copy, line)
        send_all(fc_copy, line)
        send_all(fd_copy, slabs)

    vmem = pltpu.VMEM
    dma = pltpu.SemaphoreType.DMA
    square = (ROWS, LANES)
    scratch = [
        vmem((ROWS, LANES), F32),
        vmem((3 * ROWS, LANES), F32),
        vmem((keys, ROWS), F32),
        vmem((TAPS, width), F32),
        vmem((2 * ROWS, width), F32),
        vmem((ROWS, width), BF16),
        vmem((ROWS, width), BF16),
        vmem((GROUP, 2 * ROWS, width), F32),
        vmem((ROWS, width), F32),
        vmem((ROWS, width), F32),
        vmem((ROWS, width), F32),
        vmem(square, F32),
        vmem(square, F32),
        vmem((8, ROWS), F32),
        vmem((max(1, m - 1), 8, ROWS), F32),
        vmem((2 * ROWS, width), F32),
        vmem((ROWS, width), BF16),
        vmem((ROWS, width), BF16),
        vmem((GROUP, 2 * ROWS - GROUP, LANES), F32),
        vmem((TAPS, width), F32),
        vmem((slabs, slab_taps, width), BF16),
        vmem((slabs - 1, slab_taps, width), BF16),
        vmem((line, row_taps, width), F32),
        vmem((line - 1, row_taps, width), F32),
        vmem((line, row_taps, width), F32),
        vmem((slabs, slab_taps, width), BF16),
        vmem((heads, SPAN + 1, 2, ROWS, HEAD_DIM), BF16),
        vmem((heads, 2, keys, HEAD_DIM), F32),
        vmem((heads, 2, 2, ROWS, HEAD_DIM), BF16),
        vmem((heads, 2, 2, ROWS, HEAD_DIM), BF16),
        vmem((heads, 2, ROWS, HEAD_DIM), BF16),
        vmem((heads, 2, ROWS, HEAD_DIM), BF16),
        vmem((heads, 2, ROWS, HEAD_DIM), BF16),
        vmem((heads, 2, ROWS, HEAD_DIM), BF16),
        dma((2,)),
        dma((2,)),
        dma((max(1, m - 1),)),
        dma((max(1, m - 1),)),
        dma((heads, 4)),
        dma((heads, 4)),
        dma((heads, 3)),
        dma((heads, 3)),
        dma((2, slabs - 1)),
        dma((2, slabs - 1)),
        dma((2, line - 1)),
        dma((2, line - 1)),
    ]
    return kernel, scratch


def build(mesh, line):
    n, m = mesh.shape["ctx"], mesh.shape["mp"]

    def body(aq, ak, av, ao, hq, hk, hv, ho, taps, gain, seg):
        rows, width = aq.shape
        kernel, scratch = make_kernel(n, m, width, line)
        wide = jax.ShapeDtypeStruct((rows, width), BF16)
        whole = pl.BlockSpec(memory_space=pltpu.VMEM)
        return pl.pallas_call(
            kernel,
            out_shape=(wide,) * 6 + (jax.ShapeDtypeStruct((width, TAPS), F32),),
            in_specs=[whole] * 11,
            out_specs=(whole,) * 7,
            scratch_shapes=scratch,
            compiler_params=pltpu.CompilerParams(
                collective_id=0, has_side_effects=True, vmem_limit_bytes=40 * 2**20
            ),
        )(aq, ak, av, ao, hq, hk, hv, ho, taps, gain.reshape(1, width), seg.reshape(n, rows))

    wide = P("ctx", "mp")
    return jax.shard_map(
        body,
        mesh=mesh,
        in_specs=(wide,) * 8 + (P("mp", None), P("mp"), P()),
        out_specs=(wide,) * 6 + (P("mp", None),),
        check_vma=False,
    )


def solution(mesh):
    return build(mesh, LINE)
```

time: 506 us -> 78.4 us (0.15)
  waiting for transfers between devices: 308 us -> 0 us
  other arithmetic: 77.7 us -> 0 us
  Pallas kernels: 0 us -> 63 us
  local copies, waits for them, and re-layouts: 50.2 us -> 14.3 us
  starting transfers between devices: 30.5 us -> 0 us
  between operations: 14.5 us -> 0.67 us
  blocking collectives: 8.72 us -> 0 us
  matrix products: 7.46 us -> 0 us
  loops' own time: 6.84 us -> 0 us
    psum x1 -> x0, waiting for transfers between devices: 308 us -> none  [body(): filter_grad = lax.psum(filter_terms, 'ctx') * total ** (-0.5)]
    pallas_call x0 -> x1, Pallas kernels: none -> 63 us  [body(): pl.pallas_call(kernel, out_shape=(wide,) * 6 + (jax.ShapeDtypeStruct((wid...]
    add x34 -> x0, other arithmetic: 38 us -> none  [the longest x16 30.7 us: spread_step(): return acc + jnp.where(same[:, None], piece * coeff[None, :], 0.0)]
    ppermute x10 -> x0, starting transfers between devices: 30.5 us -> none  [shifted(): lax.ppermute(value, axis, [(source, source + steps) for source in range(l...]
    eq x48 -> x0, other arithmetic: 25 us -> none  [the longest x16 12.5 us: filter_step(): same = lax.dynamic_slice_in_dim(ext_seg, rim_rows - tap, rows, 0) == own_seg]
    dynamic_slice x33 -> x0, local copies, waits for them, and re-layouts: 10.8 us -> none  [the longest x16 10.1 us: spread_step(): coeff = lax.dynamic_index_in_dim(filter_taps, tap, 1, keepdims=False)]
    psum x1 -> x0, blocking collectives: 8.72 us -> none  [body(): lax.psum((jnp.sum(gated * gated, axis=-1), jnp.sum(weighted * gated, axis...]
    gather x3 -> x0, local copies, waits for them, and re-layouts: 8.11 us -> none  [the longest x1 3.85 us: body(): key_seg = jnp.take(segment_ids, jnp.clip(key_pos, 0, total - 1))]
  transfers between devices with their start and end apart: 11 -> 0, of which waited for: 1 -> 0; matrix products, arithmetic and copies ran while one was open for 26% -> 0% of each run, Pallas kernels for 0% -> 0%
where the time goes in v1:
time: 78.4 us; the launch traced here: 78 us
  Pallas kernels  63 us (80%)
  local copies, waits for them, and re-layouts  14.3 us (18%)
    pallas_call x1, Pallas kernels, body(): pl.pallas_call(kernel, out_shape=(wide,) * 6 + (jax.ShapeDtypeStruct((wid...  63 us
    unnamed x29, local copies, waits for them, and re-layouts  14.3 us

profile of v1, /device:TPU:1, one launch (start us, length us, event | category | flops | bytes accessed | tf_op | source)
XLA Modules:
  0.0 78.0 jit_solution(9090780764487673749)
XLA Ops:
  0.6 0.0 copy-start.10
  0.6 0.7 copy-done.10
  1.3 0.0 copy-start
  1.3 0.9 %copy-done = f32[512,128]{1,0:T(8,128)S(1)} copy-done((f32[512,128]{1,0:T(8,128)S(1)}, f32[512,128]{1,0:T(8,128)}, u32[]{:S(2)}) %copy-start) | copy-done | bytes 262168
  2.3 0.0 copy-start.1
  2.3 0.9 %copy-done.1 = bf16[128,512]{1,0:T(8,128)(2,1)S(1)} copy-done((bf16[128,512]{1,0:T(8,128)(2,1)S(1)}, bf16[128,512]{1,0:T(8,128)(2,1)}, u32[]{:S(2)}) %copy-start.1) | copy-done | bytes 131096
  3.2 0.0 copy-start.2
  3.2 0.9 %copy-done.2 = bf16[128,512]{1,0:T(8,128)(2,1)S(1)} copy-done((bf16[128,512]{1,0:T(8,128)(2,1)S(1)}, bf16[128,512]{1,0:T(8,128)(2,1)}, u32[]{:S(2)}) %copy-start.2) | copy-done | bytes 131096
  4.1 0.0 copy-start.3
  4.1 0.9 %copy-done.3 = bf16[128,512]{1,0:T(8,128)(2,1)S(1)} copy-done((bf16[128,512]{1,0:T(8,128)(2,1)S(1)}, bf16[128,512]{1,0:T(8,128)(2,1)}, u32[]{:S(2)}) %copy-start.3) | copy-done | bytes 131096
  5.0 0.0 copy-start.4
  5.0 0.9 %copy-done.4 = bf16[128,512]{1,0:T(8,128)(2,1)S(1)} copy-done((bf16[128,512]{1,0:T(8,128)(2,1)S(1)}, bf16[128,512]{1,0:T(8,128)(2,1)}, u32[]{:S(2)}) %copy-start.4) | copy-done | bytes 131096
  5.9 0.0 copy-start.5
  5.9 0.9 %copy-done.5 = bf16[128,512]{1,0:T(8,128)(2,1)S(1)} copy-done((bf16[128,512]{1,0:T(8,128)(2,1)S(1)}, bf16[128,512]{1,0:T(8,128)(2,1)}, u32[]{:S(2)}) %copy-start.5) | copy-done | bytes 131096
  6.8 0.0 copy-start.6
  6.8 0.9 %copy-done.6 = bf16[128,512]{1,0:T(8,128)(2,1)S(1)} copy-done((bf16[128,512]{1,0:T(8,128)(2,1)S(1)}, bf16[128,512]{1,0:T(8,128)(2,1)}, u32[]{:S(2)}) %copy-start.6) | copy-done | bytes 131096
  7.7 0.0 copy-start.7
  7.7 0.9 %copy-done.7 = bf16[128,512]{1,0:T(8,128)(2,1)S(1)} copy-done((bf16[128,512]{1,0:T(8,128)(2,1)S(1)}, bf16[128,512]{1,0:T(8,128)(2,1)}, u32[]{:S(2)}) %copy-start.7) | copy-done | bytes 131096
  8.6 0.0 copy-start.8
  8.6 0.9 %copy-done.8 = bf16[128,512]{1,0:T(8,128)(2,1)S(1)} copy-done((bf16[128,512]{1,0:T(8,128)(2,1)S(1)}, bf16[128,512]{1,0:T(8,128)(2,1)}, u32[]{:S(2)}) %copy-start.8) | copy-done | bytes 131096
  9.5 0.0 copy-start.9
  9.5 0.8 %copy-done.9 = s32[16384]{0:T(1024)S(1)} copy-done((s32[16384]{0:T(1024)S(1)}, s32[16384]{0:T(1024)}, u32[]{:S(2)}) %copy-start.9) | copy-done | bytes 65560
  10.3 63.0 %shard_map.162 = (bf16[128,512]{1,0:T(8,128)(2,1)S(1)}, bf16[128,512]{1,0:T(8,128)(2,1)S(1)}, bf16[128,512]{1,0:T(8,128)(2,1)S(1)}, bf16[128,512]{1,0:T(8,128)(2...) custom-call(bf16[128,512]{1,0:T(8,128)(2,1)S(1)} %copy-done.1, ...), custom_call_target="tpu_custom_call" | custom-call | tf_op jit(solution)/shard_map/pallas_call | solution.py:529
  73.4 0.7 copy.25
  74.0 0.7 copy.26
  74.7 0.7 copy.27
  75.3 0.7 copy.28
  76.0 0.7 copy.29
  76.6 0.7 copy.30
  77.3 0.7 copy.31
Async XLA Ops:
  0.6 0.7 copy-start.10
  1.3 0.9 %copy-start = (f32[512,128]{1,0:T(8,128)S(1)}, f32[512,128]{1,0:T(8,128)}, u32[]{:S(2)}) copy-start(f32[512,128]{1,0:T(8,128)} %taps.1) | copy-start | bytes 786436
  2.3 0.9 %copy-start.1 = (bf16[128,512]{1,0:T(8,128)(2,1)S(1)}, bf16[128,512]{1,0:T(8,128)(2,1)}, u32[]{:S(2)}) copy-start(bf16[128,512]{1,0:T(8,128)(2,1)} %aq.1) | copy-start | bytes 393220
  3.2 0.9 %copy-start.2 = (bf16[128,512]{1,0:T(8,128)(2,1)S(1)}, bf16[128,512]{1,0:T(8,128)(2,1)}, u32[]{:S(2)}) copy-start(bf16[128,512]{1,0:T(8,128)(2,1)} %ak.1) | copy-start | bytes 393220
  4.1 0.9 %copy-start.3 = (bf16[128,512]{1,0:T(8,128)(2,1)S(1)}, bf16[128,512]{1,0:T(8,128)(2,1)}, u32[]{:S(2)}) copy-start(bf16[128,512]{1,0:T(8,128)(2,1)} %av.1) | copy-start | bytes 393220
  5.0 0.9 %copy-start.4 = (bf16[128,512]{1,0:T(8,128)(2,1)S(1)}, bf16[128,512]{1,0:T(8,128)(2,1)}, u32[]{:S(2)}) copy-start(bf16[128,512]{1,0:T(8,128)(2,1)} %ao.1) | copy-start | bytes 393220
  5.9 0.9 %copy-start.5 = (bf16[128,512]{1,0:T(8,128)(2,1)S(1)}, bf16[128,512]{1,0:T(8,128)(2,1)}, u32[]{:S(2)}) copy-start(bf16[128,512]{1,0:T(8,128)(2,1)} %hq.1) | copy-start | bytes 393220
  6.8 0.9 %copy-start.6 = (bf16[128,512]{1,0:T(8,128)(2,1)S(1)}, bf16[128,512]{1,0:T(8,128)(2,1)}, u32[]{:S(2)}) copy-start(bf16[128,512]{1,0:T(8,128)(2,1)} %hk.1) | copy-start | bytes 393220
  7.7 0.9 %copy-start.7 = (bf16[128,512]{1,0:T(8,128)(2,1)S(1)}, bf16[128,512]{1,0:T(8,128)(2,1)}, u32[]{:S(2)}) copy-start(bf16[128,512]{1,0:T(8,128)(2,1)} %hv.1) | copy-start | bytes 393220
  8.6 0.9 %copy-start.8 = (bf16[128,512]{1,0:T(8,128)(2,1)S(1)}, bf16[128,512]{1,0:T(8,128)(2,1)}, u32[]{:S(2)}) copy-start(bf16[128,512]{1,0:T(8,128)(2,1)} %ho.1) | copy-start | bytes 393220
  9.5 0.8 %copy-start.9 = (s32[16384]{0:T(1024)S(1)}, s32[16384]{0:T(1024)}, u32[]{:S(2)}) copy-start(s32[16384]{0:T(1024)} %param.21) | copy-start | bytes 196612

commit v2 on v1

v2 whole, which is shorter than its diff:
```python
import jax
import jax.numpy as jnp
from jax import lax
from jax.experimental import pallas as pl
from jax.experimental.pallas import tpu as pltpu
from jax.sharding import PartitionSpec as P

SPAN = 4
HEAD_DIM = 128
TAPS = 128
ROWS = 128
LINE = 16
GROUP = 8
QUAD = 4
PART = 64
LANES = 128
F32 = jnp.float32
BF16 = jnp.bfloat16
FAR = -1e30
MESH = pl.DeviceIdType.MESH


def contract(left, right, left_dim, right_dim):
    return lax.dot_general(
        left, right, (((left_dim,), (right_dim,)), ((), ())), preferred_element_type=F32
    )


def fold(tiles, row):
    for bit in (4, 2, 1):
        low = (row & bit) == 0
        half = len(tiles) // 2
        folded = []
        for first, second in zip(tiles[:half], tiles[half:]):
            keep = jnp.where(low, first, second)
            move = jnp.where(low, second, first)
            up = pltpu.roll(move, 8 - bit, 0)
            folded.append(keep + (up if bit == 4 else jnp.where(low, up, pltpu.roll(move, bit, 0))))
        tiles = folded
    return tiles[0]


def make_kernel(n, m, width, line):
    heads = width // HEAD_DIM
    columns = width // LANES
    channels = width * m
    pairs = line // 2
    crew = 2 * n // line
    crew_taps = TAPS // crew
    chunks = columns // 2
    keys = (SPAN + 1) * ROWS
    scale = HEAD_DIM ** (-0.5)
    pieces = ROWS // PART
    quads = TAPS // GROUP // QUAD
    inner = [piece * PART // (GROUP * QUAD) if piece else 0 for piece in range(pieces)]

    def lanes(index):
        return pl.ds(pl.multiple_of(index * LANES, LANES), LANES)

    def kernel(
        aq_in, ak_in, av_in, ao_in, hq_in, hk_in, hv_in, ho_in, taps_in, gain_in, seg_in,
        daq_out, dak_out, dav_out, dhq_out, dhk_out, dhv_out, dfilter_out,
        daq, dak, dav, dhq, dhk, dhv, dfilter,
        aq, ao, hq, hk, hv, ho, taps, gain, seg,
        segrows, segcols, bias, taps_t, ext, halo_out, halo_in, shifts,
        mixed, gated, weighted, squares, crossed, sums, sums_in,
        sig, sig_out, sig_in, back, ft, fa_out, fa_in, fb, fd,
        kv, grads, gs_out, gs_in, g2_out, g2_in, g1_out, g1_in,
        load_sem, one_send, one_recv, mp_send, mp_recv, kv_send, kv_recv,
        g_send, g_recv, f_send, f_recv, token, store_sem,
    ):
        i = lax.axis_index("ctx")
        j = lax.axis_index("mp")
        core = lax.rem(i, 2)
        chip = i // 2
        z = lax.rem(chip, line)
        x = chip // line
        pair = z // 2
        member = (x * 2 + core) * 2 + lax.rem(z, 2)
        after, before = lax.rem(i + 1, n), lax.rem(i + n - 1, n)
        ahead, behind = lax.rem(i + 2, n), lax.rem(i + n - 2, n)
        far_ahead, far_behind = lax.rem(i + 4, n), lax.rem(i + n - 4, n)
        sibling = i + 1 - 2 * core

        def copy(src, dst, send, recv, device):
            return pltpu.make_async_remote_copy(
                src_ref=src, dst_ref=dst, send_sem=send, recv_sem=recv,
                device_id=device, device_id_type=MESH,
            )

        def at_line(steps):
            return {"ctx": (x * line + lax.rem(z + line + steps, line)) * 2 + core}

        def crew_peer(step):
            other = lax.rem(member + step, crew)
            spot = (other // 4) * line + pair * 2 + lax.rem(other, 2)
            return other, {"ctx": spot * 2 + lax.rem(other // 2, 2)}

        arrays = (
            (hk_in, hk), (hv_in, hv), (taps_in, taps), (seg_in, seg), (hq_in, hq), (ho_in, ho),
            (gain_in, gain), (aq_in, aq), (ao_in, ao),
        )
        loads = [
            pltpu.make_async_copy(src, dst, load_sem.at[place])
            for place, (src, dst) in enumerate(arrays)
        ]
        for head in range(heads):
            part = slice(head * HEAD_DIM, (head + 1) * HEAD_DIM)
            for place, src in enumerate((ak_in, av_in)):
                loads.append(
                    pltpu.make_async_copy(
                        src.at[:, part], kv.at[head, 0, place], load_sem.at[len(loads)]
                    )
                )
        hk_load, hv_load, taps_load, seg_load, hq_load, ho_load, gain_load, aq_load, ao_load = loads[:9]
        kv_loads = loads[9:]
        for load in (hk_load, hv_load, *kv_loads, seg_load, taps_load):
            load.start()
        for load in (hq_load, ho_load, gain_load, aq_load, ao_load):
            load.start()

        barrier = pltpu.get_barrier_semaphore()

        def greet(device):
            pl.semaphore_signal(barrier, inc=1, device_id=device, device_id_type=MESH)

        for device in (after, before, ahead, behind, far_ahead, far_behind, sibling):
            greet({"ctx": device})
        for step in range(1, m):
            greet({"mp": lax.rem(j + step, m)})
        greet(at_line(2))
        greet(at_line(-2))

        @pl.loop(1, crew)
        def _(step):
            greet(crew_peer(step)[1])

        stores = [
            pltpu.make_async_copy(src, dst, store_sem.at[place])
            for place, (src, dst) in enumerate((
                (daq, daq_out), (dak, dak_out), (dav, dav_out), (dhq, dhq_out), (dhk, dhk_out),
                (dhv, dhv_out), (dfilter, dfilter_out),
            ))
        ]

        hk_load.wait()
        hv_load.wait()
        product = hk[...].astype(F32) * hv[...].astype(F32)
        ext[ROWS:, :] = product
        halo_out[...] = product.astype(BF16)

        pl.semaphore_wait(barrier, 7 + (m - 1) + 2 + (crew - 1))

        halo_copy = copy(halo_out, halo_in, one_send.at[0], one_recv.at[0], {"ctx": after})
        halo_copy.start()

        def own_copy(head):
            return copy(
                kv.at[head, 0], kv.at[head, 2], kv_send.at[head, 0], kv_recv.at[head, 0],
                {"ctx": ahead},
            )

        def pass_copy(head):
            return copy(
                kv.at[head, 2], kv.at[head, 4], kv_send.at[head, 1], kv_recv.at[head, 1],
                {"ctx": ahead},
            )

        def near_copy(head):
            return copy(
                kv.at[head, 2 * core], kv.at[head, 1], kv_send.at[head, 2], kv_recv.at[head, 2],
                {"ctx": sibling},
            )

        def far_copy(head):
            return copy(
                kv.at[head, 2 * core + 2], kv.at[head, 3], kv_send.at[head, 3],
                kv_recv.at[head, 3], {"ctx": sibling},
            )

        def leap_copy(head):
            return copy(
                kv.at[head, 0], kv.at[head, 4], kv_send.at[head, 1], kv_recv.at[head, 1],
                {"ctx": far_ahead},
            )

        def tell(place, steps):
            for way in (steps, -steps):
                pl.semaphore_signal(
                    token.at[place], inc=1, device_id=at_line(way), device_id_type=MESH
                )

        tell(0, 2)

        def first_service(head):
            own_copy(head).wait_recv()
            if head:
                pass_copy(head).start()
            near_copy(head).start()

        def second_service(head):
            pass_copy(head).wait_recv()
            far_copy(head).start()

        seg_load.wait()
        segrows[...] = jnp.zeros_like(segrows)
        for row in range(SPAN + 2):
            block = i - SPAN + row
            inside = (block >= 0) & (block < n)
            held = seg[pl.ds(jnp.clip(block, 0, n - 1), 1), :]
            segrows[row : row + 1, :] = jnp.where(inside, held, -1 if row < SPAN else -2).astype(F32)
        turned = segrows[...].T
        for place in range(3):
            row = SPAN - 1 + place
            segcols[place * ROWS : (place + 1) * ROWS, :] = jnp.broadcast_to(
                turned[:, row : row + 1], (ROWS, LANES)
            )

        query_seg = segrows[SPAN : SPAN + 1, :]
        key_at = lax.broadcasted_iota(jnp.int32, (ROWS, ROWS), 0)
        query_at = lax.broadcasted_iota(jnp.int32, (ROWS, ROWS), 1)
        for back_by in range(SPAN + 1):
            row = SPAN - back_by
            allowed = turned[:, row : row + 1] == query_seg
            if back_by == 0:
                allowed = allowed & (key_at <= query_at)
            bias[back_by * ROWS : (back_by + 1) * ROWS, :] = jnp.where(allowed, 0.0, FAR)

        def shift_rows(start, stop):
            @pl.loop(0, columns)
            def _(column):
                part = lanes(column)
                for r in range(GROUP):
                    same = segcols[start - r : stop - r, :] == segcols[start:stop, :]
                    shifts[r, start:stop, part] = jnp.where(
                        same, ext[start - r : stop - r, part], 0.0
                    )

        shift_rows(ROWS + GROUP, 2 * ROWS)
        taps_load.wait()
        taps_t[...] = taps[...].T
        squares[...] = jnp.zeros_like(squares)
        crossed[...] = jnp.zeros_like(crossed)
        def tap_groups(column, piece, start, stop, total):
            part = lanes(column)
            own = segcols[ROWS + piece * PART : ROWS + (piece + 1) * PART, :]
            span = PART + GROUP * (QUAD - 1)

            def step(quad, total):
                first = pl.multiple_of(
                    ROWS + piece * PART - GROUP * (QUAD * quad + QUAD - 1), GROUP
                )
                begin = pl.multiple_of(GROUP * QUAD * quad, GROUP * QUAD)
                coeff = taps_t[pl.ds(begin, GROUP * QUAD), part]
                segs = segcols[pl.ds(first, span), :]
                terms = [None] * QUAD
                for r in range(GROUP):
                    block = shifts[r, pl.ds(first, span), part]
                    for k in range(QUAD):
                        off = GROUP * (QUAD - 1 - k)
                        at = GROUP * k + r
                        term = coeff[at : at + 1] * block[off : off + PART]
                        terms[k] = term if r == 0 else terms[k] + term
                for k in range(QUAD):
                    off = GROUP * (QUAD - 1 - k)
                    total = total + jnp.where(segs[off : off + PART] == own, terms[k], 0.0)
                return total

            return lax.fori_loop(start, stop, step, total)

        def convolve(column):
            part = lanes(column)
            for piece in range(pieces):
                rows = slice(piece * PART, (piece + 1) * PART)
                if piece == 0:
                    begun = jnp.zeros((PART, LANES), F32)
                else:
                    begun = mixed[rows, part]
                found = tap_groups(column, piece, inner[piece], quads, begun)
                mixed[rows, part] = found
                gate = hq[rows, part].astype(F32) * found
                heavy = gain[:, part] * ho[rows, part].astype(F32)
                gated[rows, part] = gate
                weighted[rows, part] = heavy
                squares[rows, :] += gate * gate
                crossed[rows, :] += heavy * gate

        def attend(head):
            part = lanes(head)
            near_copy(head).wait_recv()
            far_copy(head).wait_recv()
            query, cot = aq[:, part], ao[:, part]
            key_all = kv[head, :, 0].reshape(keys, HEAD_DIM)
            value_all = kv[head, :, 1].reshape(keys, HEAD_DIM)
            scores = contract(key_all, query, 1, 1) * scale + bias[...]
            peak = jnp.max(scores, axis=0, keepdims=True)
            powers = jnp.exp(scores - peak)
            probs = powers * (1.0 / jnp.sum(powers, axis=0, keepdims=True))
            low = probs.astype(BF16)
            slope = contract(value_all, cot, 1, 1)
            offset = jnp.sum(low.astype(F32) * slope, axis=0, keepdims=True)
            score_grad = (probs * (slope - offset)).astype(BF16)
            daq[:, part] = (contract(score_grad, key_all, 0, 0) * scale).astype(BF16)
            grads[head, 0] = contract(score_grad, query, 1, 0) * scale
            grads[head, 1] = contract(low, cot, 1, 0)
            for place in range(2):
                rows = slice((2 * place + 1) * ROWS, (2 * place + 2) * ROWS)
                gs_out[head, place] = grads[head, :, rows].astype(BF16)
            gs_copy(head).start()

        def gs_copy(head):
            return copy(
                gs_out.at[head], gs_in.at[head], g_send.at[head, 0], g_recv.at[head, 0],
                {"ctx": sibling},
            )

        def g2_copy(head):
            return copy(
                g2_out.at[head], g2_in.at[head], g_send.at[head, 1], g_recv.at[head, 1],
                {"ctx": behind},
            )

        def g1_copy(head):
            return copy(
                g1_out.at[head], g1_in.at[head], g_send.at[head, 2], g_recv.at[head, 2],
                {"ctx": behind},
            )

        first_core = core == 0

        def return_two(head):
            gs_copy(head).wait_recv()
            mine = grads[head, :, 4 * ROWS : 5 * ROWS]
            theirs = gs_in[head, 1].astype(F32)
            g2_out[head] = (mine + jnp.where(first_core, 0.0, theirs)).astype(BF16)
            g2_copy(head).start()

        def return_one(head):
            g2_copy(head).wait_recv()
            mine = grads[head, :, 2 * ROWS : 3 * ROWS]
            theirs = jnp.where(first_core, gs_in[head, 1].astype(F32), gs_in[head, 0].astype(F32))
            g1_out[head] = (mine + theirs + g2_in[head].astype(F32)).astype(BF16)
            g1_copy(head).start()

        def return_own(head):
            part = lanes(head)
            g1_copy(head).wait_recv()
            mine = grads[head, :, 0:ROWS]
            theirs = jnp.where(first_core, gs_in[head, 0].astype(F32), 0.0)
            done = mine + theirs + g1_in[head].astype(F32)
            dak[:, part] = done[0].astype(BF16)
            dav[:, part] = done[1].astype(BF16)

        @pl.loop(0, columns)
        def _(column):
            for piece in range(1, pieces):
                rows = slice(piece * PART, (piece + 1) * PART)
                mixed[rows, lanes(column)] = tap_groups(
                    column, piece, 0, inner[piece], jnp.zeros((PART, LANES), F32)
                )

        for load in (*kv_loads, hq_load, ho_load, gain_load):
            load.wait()
        own_copy(0).start()
        leap_copy(0).start()
        own_copy(1).start()

        halo_copy.wait_recv()
        ext[:ROWS, :] = halo_in[...].astype(F32)
        shift_rows(GROUP, ROWS + GROUP)

        @pl.loop(0, 2)
        def _(column):
            convolve(column)

        own_copy(2).start()

        @pl.loop(2, columns)
        def _(column):
            convolve(column)

        square_sum = jnp.sum(squares[...], axis=1, keepdims=True)
        cross_sum = jnp.sum(crossed[...], axis=1, keepdims=True)
        lane_at = lax.broadcasted_iota(jnp.int32, (ROWS, LANES), 1)
        squares[...] = jnp.where(lane_at == 0, square_sum, jnp.where(lane_at == 1, cross_sum, 0.0))
        sums[...] = squares[...].T[0:8]

        def sum_copy(step):
            return copy(
                sums, sums_in.at[step - 1], mp_send.at[step - 1], mp_recv.at[step - 1],
                {"mp": lax.rem(j + step, m)},
            )

        for step in range(1, m):
            sum_copy(step).start()

        pl.semaphore_wait(token.at[0], 2)
        tell(1, 4)
        own_copy(3).start()
        first_service(0)
        second_service(0)
        first_service(1)
        aq_load.wait()
        ao_load.wait()
        attend(0)
        for step in range(1, m):
            sum_copy(step).wait_recv()
        whole = sums[...]
        for step in range(1, m):
            whole = whole + sums_in[step - 1]
        inverse = lax.rsqrt(whole[0:1] / channels + 1e-06)
        factor = inverse * inverse * inverse * (whole[1:2] / channels)
        squares[0:1, :] = inverse
        squares[1:2, :] = factor
        upright = squares[...].T
        squares[...] = jnp.broadcast_to(upright[:, 0:1], (ROWS, LANES))
        crossed[...] = jnp.broadcast_to(upright[:, 1:2], (ROWS, LANES))

        @pl.loop(0, columns)
        def _(column):
            part = lanes(column)
            slope = squares[...] * weighted[:, part] - gated[:, part] * crossed[...]
            dhq[:, part] = (slope * mixed[:, part]).astype(BF16)
            signal = slope * hq[:, part].astype(F32)
            sig[:ROWS, part] = signal
            sig_out[:, part] = signal.astype(BF16)

        sig_copy = copy(sig_out, sig_in, one_send.at[1], one_recv.at[1], {"ctx": before})
        sig_copy.start()
        stores[3].start()

        def correlate(column):
            part = lanes(column)
            own = segcols[ROWS : 2 * ROWS, :]
            signal = sig[:ROWS, part]
            row = lax.broadcasted_iota(jnp.int32, (GROUP, LANES), 0)

            @pl.loop(0, quads)
            def _(quad):
                span = PART + GROUP * (QUAD - 1)
                for piece in range(pieces):
                    rows = slice(piece * PART, (piece + 1) * PART)
                    first = pl.multiple_of(
                        ROWS + piece * PART - GROUP * (QUAD * quad + QUAD - 1), GROUP
                    )
                    segs = segcols[pl.ds(first, span), :]
                    masked = [
                        jnp.where(segs[off : off + PART] == own[rows], signal[rows], 0.0)
                        for off in range(GROUP * (QUAD - 1), -1, -GROUP)
                    ]
                    found = [[] for _ in range(QUAD)]
                    for r in range(GROUP):
                        block = shifts[r, pl.ds(first, span), part]
                        for k in range(QUAD):
                            off = GROUP * (QUAD - 1 - k)
                            term = masked[k] * block[off : off + PART]
                            found[k].append(term.reshape(PART // 8, 8, LANES).sum(axis=0))
                    for k in range(QUAD):
                        begin = pl.multiple_of(GROUP * (QUAD * quad + k), GROUP)
                        total = fold(found[k], row)
                        if piece:
                            total = total + ft[pl.ds(begin, GROUP), part]
                        ft[pl.ds(begin, GROUP), part] = total

        def fa_copy(chunk, step):
            other, device = crew_peer(step)
            return copy(
                fa_out.at[chunk, other], fa_in.at[chunk, step - 1], f_send.at[0, chunk],
                f_recv.at[0, chunk], device,
            )

        def fb_copy(chunk, step):
            return copy(
                fb.at[chunk, pair], fb.at[chunk, pair], f_send.at[1, chunk],
                f_recv.at[1, chunk], at_line(2 * step),
            )

        def fd_copy(chunk, step):
            _, device = crew_peer(step)
            return copy(
                fd.at[chunk, member], fd.at[chunk, member], f_send.at[2, chunk],
                f_recv.at[2, chunk], device,
            )

        def wait_bytes(held, sems, phase, chunk, count):
            ref = held.at[chunk, pl.ds(0, count)]
            pltpu.make_async_copy(ref, ref, sems.at[phase, chunk]).wait()

        def start_all(make, chunk, count):
            @pl.loop(1, count)
            def _(step):
                make(chunk, step).start()

        def filter_out(chunk):
            for owner in range(crew):
                rows = slice(owner * crew_taps, (owner + 1) * crew_taps)
                tile = [ft[rows, lanes(2 * chunk + side)] for side in range(2)]
                fa_out[chunk, owner] = jnp.concatenate(tile).astype(BF16)
            start_all(fa_copy, chunk, crew)

        def filter_sum(chunk):
            wait_bytes(fa_in, f_recv, 0, chunk, crew - 1)
            rows = pl.ds(pl.multiple_of(member * crew_taps, crew_taps), crew_taps)
            total = jnp.concatenate([ft[rows, lanes(2 * chunk + side)] for side in range(2)])
            for step in range(1, crew):
                total = total + fa_in[chunk, step - 1].astype(F32)
            fb[chunk, pair] = total.astype(BF16)
            start_all(fb_copy, chunk, pairs)

        def filter_whole(chunk):
            wait_bytes(fb, f_recv, 1, chunk, pairs - 1)
            total = fb[chunk, 0].astype(F32)
            for place in range(1, pairs):
                total = total + fb[chunk, place].astype(F32)
            fd[chunk, member] = (total * (n * ROWS) ** (-0.5)).astype(BF16)
            start_all(fd_copy, chunk, crew)

        def filter_done(chunk):
            wait_bytes(fd, f_recv, 2, chunk, crew - 1)
            for side in range(2):
                rows = slice(side * crew_taps, (side + 1) * crew_taps)
                taps_row = fd[chunk, :, rows].astype(F32).reshape(TAPS, LANES)
                begin = (2 * chunk + side) * LANES
                dfilter[begin : begin + LANES, :] = taps_row.T

        def spread(column):
            part = lanes(column)
            reach = 2 * ROWS - GROUP
            for r in range(GROUP):
                same = segcols[ROWS + r : ROWS + r + reach, :] == segcols[ROWS : ROWS + reach, :]
                back[r] = jnp.where(same, sig[r : r + reach, part], 0.0)
            for piece in range(ROWS // PART):
                rows = slice(piece * PART, (piece + 1) * PART)
                own = segcols[ROWS + piece * PART : ROWS + (piece + 1) * PART, :]
                span = PART + GROUP * (QUAD - 1)

                def step(quad, total):
                    begin = pl.multiple_of(GROUP * QUAD * quad, GROUP * QUAD)
                    first = pl.multiple_of(piece * PART + begin, GROUP)
                    coeff = taps_t[pl.ds(begin, GROUP * QUAD), part]
                    segs = segcols[pl.ds(pl.multiple_of(ROWS + first, GROUP), span), :]
                    terms = [None] * QUAD
                    for r in range(GROUP):
                        block = back[r, pl.ds(first, span), :]
                        for k in range(QUAD):
                            at = GROUP * k + r
                            term = coeff[at : at + 1] * block[GROUP * k : GROUP * k + PART]
                            terms[k] = term if r == 0 else terms[k] + term
                    for k in range(QUAD):
                        same = segs[GROUP * k : GROUP * k + PART] == own
                        total = total + jnp.where(same, terms[k], 0.0)
                    return total

                found = lax.fori_loop(
                    0, TAPS // GROUP // QUAD, step, jnp.zeros((PART, LANES), F32)
                )
                dhk[rows, part] = (found * hv[rows, part].astype(F32)).astype(BF16)
                dhv[rows, part] = (found * hk[rows, part].astype(F32)).astype(BF16)

        correlate(0)
        first_service(2)
        return_two(0)
        correlate(1)
        filter_out(0)
        first_service(3)
        second_service(1)
        correlate(2)
        correlate(3)
        filter_out(1)
        second_service(2)
        return_one(0)
        attend(1)
        second_service(3)
        pl.semaphore_wait(token.at[1], 2)
        filter_sum(0)
        attend(2)
        return_two(1)
        sig_copy.wait_recv()
        sig[ROWS:, :] = sig_in[...].astype(F32)
        spread(0)
        return_two(2)
        filter_sum(1)
        attend(3)
        stores[0].start()
        return_one(1)
        spread(1)
        return_two(3)
        return_one(2)
        spread(2)
        spread(3)
        stores[4].start()
        stores[5].start()
        return_one(3)
        filter_whole(0)
        return_own(0)
        return_own(1)
        filter_whole(1)
        return_own(2)
        return_own(3)
        stores[1].start()
        stores[2].start()
        filter_done(0)
        filter_done(1)
        stores[6].start()

        halo_copy.wait_send()
        sig_copy.wait_send()
        for step in range(1, m):
            sum_copy(step).wait_send()

        @pl.loop(0, heads)
        def _(head):
            for made in (own_copy, pass_copy, near_copy, far_copy, gs_copy, g2_copy, g1_copy):
                made(head).wait_send()

        for chunk in range(chunks):
            wait_bytes(fa_in, f_send, 0, chunk, crew - 1)
            wait_bytes(fb, f_send, 1, chunk, pairs - 1)
            wait_bytes(fd, f_send, 2, chunk, crew - 1)
        for store in stores:
            store.wait()

    vmem = pltpu.VMEM
    dma = pltpu.SemaphoreType.DMA
    square = (ROWS, LANES)
    wide = vmem((ROWS, width), BF16)
    scratch = [
        wide, wide, wide, wide, wide, wide,
        vmem((width, TAPS), F32),
        wide, wide, wide, wide, wide, wide,
        vmem((width, TAPS), F32),
        vmem((1, width), F32),
        vmem((n, ROWS), jnp.int32),
        vmem((ROWS, LANES), F32),
        vmem((3 * ROWS, LANES), F32),
        vmem((keys, ROWS), F32),
        vmem((TAPS, width), F32),
        vmem((2 * ROWS, width), F32),
        wide,
        wide,
        vmem((GROUP, 2 * ROWS, width), F32),
        vmem((ROWS, width), F32),
        vmem((ROWS, width), F32),
        vmem((ROWS, width), F32),
        vmem(square, F32),
        vmem(square, F32),
        vmem((8, ROWS), F32),
        vmem((max(1, m - 1), 8, ROWS), F32),
        vmem((2 * ROWS, width), F32),
        wide,
        wide,
        vmem((GROUP, 2 * ROWS - GROUP, LANES), F32),
        vmem((TAPS, width), F32),
        vmem((chunks, crew, 2 * crew_taps, LANES), BF16),
        vmem((chunks, crew - 1, 2 * crew_taps, LANES), BF16),
        vmem((chunks, pairs, 2 * crew_taps, LANES), BF16),
        vmem((chunks, crew, 2 * crew_taps, LANES), BF16),
        vmem((heads, SPAN + 1, 2, ROWS, HEAD_DIM), BF16),
        vmem((heads, 2, keys, HEAD_DIM), F32),
        vmem((heads, 2, 2, ROWS, HEAD_DIM), BF16),
        vmem((heads, 2, 2, ROWS, HEAD_DIM), BF16),
        vmem((heads, 2, ROWS, HEAD_DIM), BF16),
        vmem((heads, 2, ROWS, HEAD_DIM), BF16),
        vmem((heads, 2, ROWS, HEAD_DIM), BF16),
        vmem((heads, 2, ROWS, HEAD_DIM), BF16),
        dma((9 + 2 * heads,)),
        dma((2,)),
        dma((2,)),
        dma((max(1, m - 1),)),
        dma((max(1, m - 1),)),
        dma((heads, 4)),
        dma((heads, 4)),
        dma((heads, 3)),
        dma((heads, 3)),
        dma((3, chunks)),
        dma((3, chunks)),
        pltpu.SemaphoreType.REGULAR((2,)),
        dma((7,)),
    ]
    return kernel, scratch


def write_out(*refs):
    count = (len(refs) - 1) // 3
    sources, results, held, sems = refs[:count], refs[count : 2 * count], refs[2 * count : -1], refs[-1]
    loads = [
        pltpu.make_async_copy(src, mid, sems.at[0, place])
        for place, (src, mid) in enumerate(zip(sources, held))
    ]
    stores = [
        pltpu.make_async_copy(mid, dst, sems.at[1, place])
        for place, (mid, dst) in enumerate(zip(held, results))
    ]
    for load in loads:
        load.start()
    for load, store in zip(loads, stores):
        load.wait()
        store.start()
    for store in stores:
        store.wait()


def build(mesh, line):
    n, m = mesh.shape["ctx"], mesh.shape["mp"]

    def body(aq, ak, av, ao, hq, hk, hv, ho, taps, gain, seg):
        rows, width = aq.shape
        kernel, scratch = make_kernel(n, m, width, line)
        wide = jax.ShapeDtypeStruct((rows, width), BF16)
        shapes = (wide,) * 6 + (jax.ShapeDtypeStruct((width, TAPS), F32),)
        far = pl.BlockSpec(memory_space=pltpu.HBM)
        found = pl.pallas_call(
            kernel,
            out_shape=shapes,
            in_specs=[far] * 11,
            out_specs=(far,) * 7,
            scratch_shapes=scratch,
            compiler_params=pltpu.CompilerParams(
                collective_id=0, has_side_effects=True, vmem_limit_bytes=60 * 2**20
            ),
        )(aq, ak, av, ao, hq, hk, hv, ho, taps, gain.reshape(1, width), seg.reshape(n, rows))
        return pl.pallas_call(
            write_out,
            out_shape=shapes,
            in_specs=[far] * 7,
            out_specs=(far,) * 7,
            scratch_shapes=[pltpu.VMEM(one.shape, one.dtype) for one in shapes]
            + [pltpu.SemaphoreType.DMA((2, 7))],
            compiler_params=pltpu.CompilerParams(vmem_limit_bytes=60 * 2**20),
        )(*found)

    wide = P("ctx", "mp")
    return jax.shard_map(
        body,
        mesh=mesh,
        in_specs=(wide,) * 8 + (P("mp", None), P("mp"), P()),
        out_specs=(wide,) * 6 + (P("mp", None),),
        check_vma=False,
    )


def solution(mesh):
    return build(mesh, LINE)
```

time: 78.4 us -> 53.1 us (0.68)
  local copies, waits for them, and re-layouts: 14.3 us -> 0 us
  Pallas kernels: 63 us -> 52.3 us
    unnamed x29 -> x0, local copies, waits for them, and re-layouts: 14.3 us -> none
    pallas_call x1 -> x2, Pallas kernels: 63 us -> 52.3 us  [the longest x1 50.1 us: body(): pl.pallas_call(kernel, out_shape=shapes, in_specs=[far] * 11, out_specs=(...]
where the time goes in v2:
time: 53.1 us; the launch traced here: 52.9 us
  Pallas kernels  52.3 us (98%)
  between operations  0.64 us (1%)
    pallas_call x1, Pallas kernels, body(): pl.pallas_call(kernel, out_shape=shapes, in_specs=[far] * 11, out_specs=(...  50.1 us
    pallas_call x1, Pallas kernels, body(): pl.pallas_call(write_out, out_shape=shapes, in_specs=[far] * 7, out_specs...  2.12 us

profile of v2, /device:TPU:1, one launch (start us, length us, event | category | flops | bytes accessed | tf_op | source)
XLA Modules:
  0.0 52.9 jit_solution(16818995863462725585)
XLA Ops:
  0.6 50.1 %shard_map.162 = (bf16[128,512]{1,0:T(8,128)(2,1)}, bf16[128,512]{1,0:T(8,128)(2,1)}, bf16[128,512]{1,0:T(8,128)(2,1)}, bf16[128,512]{1,0:T(8,128)(2,1)}, bf16[1...) custom-call(bf16[128,512]{1,0:T(8,128)(2,1)} %aq_in.1, bf16[128,512]{1,0:T(8,128)(2,1)} %ak_in.1, ...), custom_call_target="tpu_custom_call" | custom-call | tf_op jit(solution)/shard_map/pallas_call | solution.py:712
  50.8 2.1 %shard_map.163 = (bf16[128,512]{1,0:T(8,128)(2,1)}, bf16[128,512]{1,0:T(8,128)(2,1)}, bf16[128,512]{1,0:T(8,128)(2,1)}, bf16[128,512]{1,0:T(8,128)(2,1)}, bf16[1...) custom-call(bf16[128,512]{1,0:T(8,128)(2,1)} %get-tuple-element.14.refs_0_, ...), custom_call_target="tpu_custom_call" | custom-call | tf_op jit(solution)/shard_map/pallas_call | solution.py:722

commit v3 on v2

--- a/solution.py
+++ b/solution.py
@@ -47,7 +47,8 @@
     pairs = line // 2
     crew = 2 * n // line
     crew_taps = TAPS // crew
-    chunks = columns // 2
+    chunks = 1
+    sides = columns // chunks
     keys = (SPAN + 1) * ROWS
     scale = HEAD_DIM ** (-0.5)
     pieces = ROWS // PART
@@ -61,11 +62,11 @@
         aq_in, ak_in, av_in, ao_in, hq_in, hk_in, hv_in, ho_in, taps_in, gain_in, seg_in,
         daq_out, dak_out, dav_out, dhq_out, dhk_out, dhv_out, dfilter_out,
         daq, dak, dav, dhq, dhk, dhv, dfilter,
-        aq, ao, hq, hk, hv, ho, taps, gain, seg,
+        hq, hk, hv, ho, taps, gain, seg,
         segrows, segcols, bias, taps_t, ext, halo_out, halo_in, shifts,
         mixed, gated, weighted, squares, crossed, sums, sums_in,
         sig, sig_out, sig_in, back, ft, fa_out, fa_in, fb, fd,
-        kv, grads, gs_out, gs_in, g2_out, g2_in, g1_out, g1_in,
+        kv, qc, qc_in, dq_out, dq_in, grads, gs_out, gs_in, up_out, up_in, down_out, down_in,
         load_sem, one_send, one_recv, mp_send, mp_recv, kv_send, kv_recv,
         g_send, g_recv, f_send, f_recv, token, store_sem,
     ):
@@ -79,7 +80,6 @@
         member = (x * 2 + core) * 2 + lax.rem(z, 2)
         after, before = lax.rem(i + 1, n), lax.rem(i + n - 1, n)
         ahead, behind = lax.rem(i + 2, n), lax.rem(i + n - 2, n)
-        far_ahead, far_behind = lax.rem(i + 4, n), lax.rem(i + n - 4, n)
         sibling = i + 1 - 2 * core
 
         def copy(src, dst, send, recv, device):
@@ -98,7 +98,7 @@
 
         arrays = (
             (hk_in, hk), (hv_in, hv), (taps_in, taps), (seg_in, seg), (hq_in, hq), (ho_in, ho),
-            (gain_in, gain), (aq_in, aq), (ao_in, ao),
+            (gain_in, gain),
         )
         loads = [
             pltpu.make_async_copy(src, dst, load_sem.at[place])
@@ -106,35 +106,46 @@
         ]
         for head in range(heads):
             part = slice(head * HEAD_DIM, (head + 1) * HEAD_DIM)
-            for place, src in enumerate((ak_in, av_in)):
-                loads.append(
-                    pltpu.make_async_copy(
-                        src.at[:, part], kv.at[head, 0, place], load_sem.at[len(loads)]
-                    )
-                )
-        hk_load, hv_load, taps_load, seg_load, hq_load, ho_load, gain_load, aq_load, ao_load = loads[:9]
-        kv_loads = loads[9:]
-        for load in (hk_load, hv_load, *kv_loads, seg_load, taps_load):
+            for src, dst in (
+                (ak_in, kv.at[head, 2, 0]), (av_in, kv.at[head, 2, 1]),
+                (aq_in, qc.at[head, 0]), (ao_in, qc.at[head, 1]),
+            ):
+                loads.append(pltpu.make_async_copy(src.at[:, part], dst, load_sem.at[len(loads)]))
+        hk_load, hv_load, taps_load, seg_load, hq_load, ho_load, gain_load = loads[:7]
+        head_loads = [loads[7 + 4 * head : 11 + 4 * head] for head in range(heads)]
+        hk_load.start()
+        hv_load.start()
+
+        def at_x(steps):
+            wide = crew // 4
+            return {"ctx": (lax.rem(x + wide + steps, wide) * line + z) * 2 + core}
+
+        def at_mp(steps):
+            return {"mp": lax.rem(j + m + steps, m)}
+
+        beside = [{"ctx": sibling}, at_line(1), at_line(-1)]
+        if crew > 4:
+            beside += [at_x(1), at_x(-1)]
+        across = [at_mp(1), at_mp(-1)] if m > 1 else []
+        greeted = beside + across + [{"ctx": one} for one in (after, before, ahead, behind)]
+        rounds = [
+            beside + across,
+            beside + [at_line(2), at_line(-2)],
+            [{"ctx": sibling}, at_line(4), at_line(-4)],
+        ]
+        barrier = pltpu.get_barrier_semaphore()
+        for device in greeted:
+            pl.semaphore_signal(barrier, inc=1, device_id=device, device_id_type=MESH)
+
+        def tell(place):
+            for device in rounds[place]:
+                pl.semaphore_signal(token.at[place], inc=1, device_id=device, device_id_type=MESH)
+
+        def hear(place):
+            pl.semaphore_wait(token.at[place], len(rounds[place]))
+
+        for load in (*head_loads[0], *head_loads[1]):
             load.start()
-        for load in (hq_load, ho_load, gain_load, aq_load, ao_load):
-            load.start()
-
-        barrier = pltpu.get_barrier_semaphore()
-
-        def greet(device):
-            pl.semaphore_signal(barrier, inc=1, device_id=device, device_id_type=MESH)
-
-        for device in (after, before, ahead, behind, far_ahead, far_behind, sibling):
-            greet({"ctx": device})
-        for step in range(1, m):
-            greet({"mp": lax.rem(j + step, m)})
-        greet(at_line(2))
-        greet(at_line(-2))
-
-        @pl.loop(1, crew)
-        def _(step):
-            greet(crew_peer(step)[1])
-
         stores = [
             pltpu.make_async_copy(src, dst, store_sem.at[place])
             for place, (src, dst) in enumerate((
@@ -143,75 +154,86 @@
             ))
         ]
 
+
         hk_load.wait()
         hv_load.wait()
         product = hk[...].astype(F32) * hv[...].astype(F32)
         ext[ROWS:, :] = product
-        halo_out[...] = product.astype(BF16)
-
-        pl.semaphore_wait(barrier, 7 + (m - 1) + 2 + (crew - 1))
-
-        halo_copy = copy(halo_out, halo_in, one_send.at[0], one_recv.at[0], {"ctx": after})
-        halo_copy.start()
-
-        def own_copy(head):
-            return copy(
-                kv.at[head, 0], kv.at[head, 2], kv_send.at[head, 0], kv_recv.at[head, 0],
+        for half in range(2):
+            part = slice(half * width // 2, (half + 1) * width // 2)
+            halo_out[half] = product[:, part].astype(BF16)
+
+        pl.semaphore_wait(barrier, len(greeted))
+
+        def halo_copy(half):
+            return copy(
+                halo_out.at[half], halo_in.at[half], one_send.at[half], one_recv.at[half],
+                {"ctx": after},
+            )
+
+        halo_copy(0).start()
+        halo_copy(1).start()
+        for load in (seg_load, taps_load, *loads[15:], hq_load, ho_load, gain_load):
+            load.start()
+
+        def give_back(head):
+            return copy(
+                kv.at[head, 2], kv.at[head, 0], kv_send.at[head, 0], kv_recv.at[head, 0],
+                {"ctx": behind},
+            )
+
+        def give_queries(head):
+            return copy(
+                qc.at[head], qc_in.at[head], kv_send.at[head, 1], kv_recv.at[head, 1],
+                {"ctx": behind},
+            )
+
+        def give_on(head):
+            return copy(
+                kv.at[head, 2], kv.at[head, 4], kv_send.at[head, 2], kv_recv.at[head, 2],
                 {"ctx": ahead},
             )
 
-        def pass_copy(head):
-            return copy(
-                kv.at[head, 2], kv.at[head, 4], kv_send.at[head, 1], kv_recv.at[head, 1],
-                {"ctx": ahead},
-            )
-
         def near_copy(head):
             return copy(
-                kv.at[head, 2 * core], kv.at[head, 1], kv_send.at[head, 2], kv_recv.at[head, 2],
+                kv.at[head, 2 * core], kv.at[head, 1], kv_send.at[head, 3], kv_recv.at[head, 3],
                 {"ctx": sibling},
             )
 
         def far_copy(head):
             return copy(
-                kv.at[head, 2 * core + 2], kv.at[head, 3], kv_send.at[head, 3],
-                kv_recv.at[head, 3], {"ctx": sibling},
-            )
-
-        def leap_copy(head):
-            return copy(
-                kv.at[head, 0], kv.at[head, 4], kv_send.at[head, 1], kv_recv.at[head, 1],
-                {"ctx": far_ahead},
-            )
-
-        def tell(place, steps):
-            for way in (steps, -steps):
-                pl.semaphore_signal(
-                    token.at[place], inc=1, device_id=at_line(way), device_id_type=MESH
-                )
-
-        tell(0, 2)
-
-        def first_service(head):
-            own_copy(head).wait_recv()
-            if head:
-                pass_copy(head).start()
+                kv.at[head, 2 * core + 2], kv.at[head, 3], kv_send.at[head, 4],
+                kv_recv.at[head, 4], {"ctx": sibling},
+            )
+
+        def send_back(head):
+            for load in head_loads[head]:
+                load.wait()
+            give_back(head).start()
+            give_queries(head).start()
+
+        send_back(0)
+
+        tell(0)
+
+        def service(head):
+            give_back(head).wait_recv()
+            give_on(head).wait_recv()
             near_copy(head).start()
-
-        def second_service(head):
-            pass_copy(head).wait_recv()
             far_copy(head).start()
 
         seg_load.wait()
         segrows[...] = jnp.zeros_like(segrows)
-        for row in range(SPAN + 2):
-            block = i - SPAN + row
+        asked = lax.rem(i + 2, n)
+        spots = [asked - back_by for back_by in range(SPAN, -1, -1)] + [i - 1, i, i + 1]
+        for row, block in enumerate(spots):
             inside = (block >= 0) & (block < n)
             held = seg[pl.ds(jnp.clip(block, 0, n - 1), 1), :]
-            segrows[row : row + 1, :] = jnp.where(inside, held, -1 if row < SPAN else -2).astype(F32)
+            outside = -2 if row == SPAN + 3 else -1
+            segrows[row : row + 1, :] = jnp.where(inside, held, outside).astype(F32)
         turned = segrows[...].T
         for place in range(3):
-            row = SPAN - 1 + place
+            row = SPAN + 1 + place
             segcols[place * ROWS : (place + 1) * ROWS, :] = jnp.broadcast_to(
                 turned[:, row : row + 1], (ROWS, LANES)
             )
@@ -226,8 +248,8 @@
                 allowed = allowed & (key_at <= query_at)
             bias[back_by * ROWS : (back_by + 1) * ROWS, :] = jnp.where(allowed, 0.0, FAR)
 
-        def shift_rows(start, stop):
-            @pl.loop(0, columns)
+        def shift_rows(start, stop, begin, end):
+            @pl.loop(begin, end)
             def _(column):
                 part = lanes(column)
                 for r in range(GROUP):
@@ -236,7 +258,7 @@
                         same, ext[start - r : stop - r, part], 0.0
                     )
 
-        shift_rows(ROWS + GROUP, 2 * ROWS)
+        shift_rows(ROWS + GROUP, 2 * ROWS, 0, columns)
         taps_load.wait()
         taps_t[...] = taps[...].T
         squares[...] = jnp.zeros_like(squares)
@@ -286,10 +308,10 @@
                 crossed[rows, :] += heavy * gate
 
         def attend(head):
-            part = lanes(head)
             near_copy(head).wait_recv()
             far_copy(head).wait_recv()
-            query, cot = aq[:, part], ao[:, part]
+            give_queries(head).wait_recv()
+            query, cot = qc_in[head, 0], qc_in[head, 1]
             key_all = kv[head, :, 0].reshape(keys, HEAD_DIM)
             value_all = kv[head, :, 1].reshape(keys, HEAD_DIM)
             scores = contract(key_all, query, 1, 1) * scale + bias[...]
@@ -300,7 +322,7 @@
             slope = contract(value_all, cot, 1, 1)
             offset = jnp.sum(low.astype(F32) * slope, axis=0, keepdims=True)
             score_grad = (probs * (slope - offset)).astype(BF16)
-            daq[:, part] = (contract(score_grad, key_all, 0, 0) * scale).astype(BF16)
+            dq_out[head] = (contract(score_grad, key_all, 0, 0) * scale).astype(BF16)
             grads[head, 0] = contract(score_grad, query, 1, 0) * scale
             grads[head, 1] = contract(low, cot, 1, 0)
             for place in range(2):
@@ -314,40 +336,47 @@
                 {"ctx": sibling},
             )
 
-        def g2_copy(head):
-            return copy(
-                g2_out.at[head], g2_in.at[head], g_send.at[head, 1], g_recv.at[head, 1],
+        def dq_copy(head):
+            return copy(
+                dq_out.at[head], dq_in.at[head], g_send.at[head, 1], g_recv.at[head, 1],
+                {"ctx": ahead},
+            )
+
+        def up_copy(head):
+            return copy(
+                up_out.at[head], up_in.at[head], g_send.at[head, 2], g_recv.at[head, 2],
+                {"ctx": ahead},
+            )
+
+        def down_copy(head):
+            return copy(
+                down_out.at[head], down_in.at[head], g_send.at[head, 3], g_recv.at[head, 3],
                 {"ctx": behind},
             )
 
-        def g1_copy(head):
-            return copy(
-                g1_out.at[head], g1_in.at[head], g_send.at[head, 2], g_recv.at[head, 2],
-                {"ctx": behind},
-            )
-
         first_core = core == 0
 
-        def return_two(head):
+        def give_grads(head):
             gs_copy(head).wait_recv()
-            mine = grads[head, :, 4 * ROWS : 5 * ROWS]
-            theirs = gs_in[head, 1].astype(F32)
-            g2_out[head] = (mine + jnp.where(first_core, 0.0, theirs)).astype(BF16)
-            g2_copy(head).start()
-
-        def return_one(head):
-            g2_copy(head).wait_recv()
-            mine = grads[head, :, 2 * ROWS : 3 * ROWS]
+            near = gs_in[head, 0].astype(F32)
+            far = gs_in[head, 1].astype(F32)
+            ours = grads[head, :, 0:ROWS]
+            up_out[head] = (ours + jnp.where(first_core, near, 0.0)).astype(BF16)
+            up_copy(head).start()
+            ours = grads[head, :, 4 * ROWS : 5 * ROWS]
+            down_out[head] = (ours + jnp.where(first_core, 0.0, far)).astype(BF16)
+            down_copy(head).start()
+            dq_copy(head).start()
+
+        def take_grads(head):
+            part = slice(head * HEAD_DIM, (head + 1) * HEAD_DIM)
+            ours = grads[head, :, 2 * ROWS : 3 * ROWS]
             theirs = jnp.where(first_core, gs_in[head, 1].astype(F32), gs_in[head, 0].astype(F32))
-            g1_out[head] = (mine + theirs + g2_in[head].astype(F32)).astype(BF16)
-            g1_copy(head).start()
-
-        def return_own(head):
-            part = lanes(head)
-            g1_copy(head).wait_recv()
-            mine = grads[head, :, 0:ROWS]
-            theirs = jnp.where(first_core, gs_in[head, 0].astype(F32), 0.0)
-            done = mine + theirs + g1_in[head].astype(F32)
+            down_copy(head).wait_recv()
+            up_copy(head).wait_recv()
+            dq_copy(head).wait_recv()
+            done = ours + theirs + up_in[head].astype(F32) + down_in[head].astype(F32)
+            daq[:, part] = dq_in[head]
             dak[:, part] = done[0].astype(BF16)
             dav[:, part] = done[1].astype(BF16)
 
@@ -359,25 +388,28 @@
                     column, piece, 0, inner[piece], jnp.zeros((PART, LANES), F32)
                 )
 
-        for load in (*kv_loads, hq_load, ho_load, gain_load):
+        for load in (hq_load, ho_load, gain_load):
             load.wait()
-        own_copy(0).start()
-        leap_copy(0).start()
-        own_copy(1).start()
-
-        halo_copy.wait_recv()
-        ext[:ROWS, :] = halo_in[...].astype(F32)
-        shift_rows(GROUP, ROWS + GROUP)
-
-        @pl.loop(0, 2)
-        def _(column):
-            convolve(column)
-
-        own_copy(2).start()
-
-        @pl.loop(2, columns)
-        def _(column):
-            convolve(column)
+        give_on(0).start()
+        send_back(1)
+        hear(0)
+        tell(1)
+
+        for half in range(2):
+            part = slice(half * width // 2, (half + 1) * width // 2)
+            halo_copy(half).wait_recv()
+            if half == 0:
+                give_on(1).start()
+            else:
+                send_back(2)
+                give_on(2).start()
+            ext[:ROWS, part] = halo_in[half].astype(F32)
+            begin, end = half * columns // 2, (half + 1) * columns // 2
+            shift_rows(GROUP, ROWS + GROUP, begin, end)
+
+            @pl.loop(begin, end)
+            def _(column):
+                convolve(column)
 
         square_sum = jnp.sum(squares[...], axis=1, keepdims=True)
         cross_sum = jnp.sum(crossed[...], axis=1, keepdims=True)
@@ -394,14 +426,11 @@
         for step in range(1, m):
             sum_copy(step).start()
 
-        pl.semaphore_wait(token.at[0], 2)
-        tell(1, 4)
-        own_copy(3).start()
-        first_service(0)
-        second_service(0)
-        first_service(1)
-        aq_load.wait()
-        ao_load.wait()
+        hear(1)
+        tell(2)
+        send_back(3)
+        give_on(3).start()
+        service(0)
         attend(0)
         for step in range(1, m):
             sum_copy(step).wait_recv()
@@ -425,10 +454,9 @@
             sig[:ROWS, part] = signal
             sig_out[:, part] = signal.astype(BF16)
 
-        sig_copy = copy(sig_out, sig_in, one_send.at[1], one_recv.at[1], {"ctx": before})
+        sig_copy = copy(sig_out, sig_in, one_send.at[2], one_recv.at[2], {"ctx": before})
         sig_copy.start()
         stores[3].start()
-
         def correlate(column):
             part = lanes(column)
             own = segcols[ROWS : 2 * ROWS, :]
@@ -494,18 +522,20 @@
         def filter_out(chunk):
             for owner in range(crew):
                 rows = slice(owner * crew_taps, (owner + 1) * crew_taps)
-                tile = [ft[rows, lanes(2 * chunk + side)] for side in range(2)]
+                tile = [ft[rows, lanes(sides * chunk + side)] for side in range(sides)]
                 fa_out[chunk, owner] = jnp.concatenate(tile).astype(BF16)
             start_all(fa_copy, chunk, crew)
 
         def filter_sum(chunk):
             wait_bytes(fa_in, f_recv, 0, chunk, crew - 1)
             rows = pl.ds(pl.multiple_of(member * crew_taps, crew_taps), crew_taps)
-            total = jnp.concatenate([ft[rows, lanes(2 * chunk + side)] for side in range(2)])
+            tile = [ft[rows, lanes(sides * chunk + side)] for side in range(sides)]
+            total = jnp.concatenate(tile)
             for step in range(1, crew):
                 total = total + fa_in[chunk, step - 1].astype(F32)
             fb[chunk, pair] = total.astype(BF16)
-            start_all(fb_copy, chunk, pairs)
+            for step in sorted(range(1, pairs), key=lambda step: -min(step, pairs - step)):
+                fb_copy(chunk, step).start()
 
         def filter_whole(chunk):
             wait_bytes(fb, f_recv, 1, chunk, pairs - 1)
@@ -517,10 +547,10 @@
 
         def filter_done(chunk):
             wait_bytes(fd, f_recv, 2, chunk, crew - 1)
-            for side in range(2):
+            for side in range(sides):
                 rows = slice(side * crew_taps, (side + 1) * crew_taps)
                 taps_row = fd[chunk, :, rows].astype(F32).reshape(TAPS, LANES)
-                begin = (2 * chunk + side) * LANES
+                begin = (sides * chunk + side) * LANES
                 dfilter[begin : begin + LANES, :] = taps_row.T
 
         def spread(column):
@@ -558,65 +588,56 @@
                 dhv[rows, part] = (found * hk[rows, part].astype(F32)).astype(BF16)
 
         correlate(0)
-        first_service(2)
-        return_two(0)
+        give_grads(0)
+        service(1)
         correlate(1)
-        filter_out(0)
-        first_service(3)
-        second_service(1)
+        service(2)
         correlate(2)
         correlate(3)
-        filter_out(1)
-        second_service(2)
-        return_one(0)
+        hear(2)
+        filter_out(0)
         attend(1)
-        second_service(3)
-        pl.semaphore_wait(token.at[1], 2)
+        service(3)
+        attend(2)
+        give_grads(1)
+        attend(3)
         filter_sum(0)
-        attend(2)
-        return_two(1)
+        give_grads(2)
         sig_copy.wait_recv()
         sig[ROWS:, :] = sig_in[...].astype(F32)
         spread(0)
-        return_two(2)
-        filter_sum(1)
-        attend(3)
-        stores[0].start()
-        return_one(1)
+        give_grads(3)
         spread(1)
-        return_two(3)
-        return_one(2)
         spread(2)
         spread(3)
         stores[4].start()
         stores[5].start()
-        return_one(3)
+        take_grads(0)
         filter_whole(0)
-        return_own(0)
-        return_own(1)
-        filter_whole(1)
-        return_own(2)
-        return_own(3)
-        stores[1].start()
-        stores[2].start()
-        filter_done(0)
-        filter_done(1)
-        stores[6].start()
-
-        halo_copy.wait_send()
+        take_grads(1)
+        take_grads(2)
+        take_grads(3)
+        for place in range(3):
+            stores[place].start()
+
+        halo_copy(0).wait_send()
+        halo_copy(1).wait_send()
         sig_copy.wait_send()
         for step in range(1, m):
             sum_copy(step).wait_send()
-
-        @pl.loop(0, heads)
-        def _(head):
-            for made in (own_copy, pass_copy, near_copy, far_copy, gs_copy, g2_copy, g1_copy):
+        for head in range(heads):
+            for made in (
+                give_back, give_queries, give_on, near_copy, far_copy, gs_copy, dq_copy, up_copy,
+                down_copy,
+            ):
                 made(head).wait_send()
-
         for chunk in range(chunks):
             wait_bytes(fa_in, f_send, 0, chunk, crew - 1)
             wait_bytes(fb, f_send, 1, chunk, pairs - 1)
+        for chunk in range(chunks):
+            filter_done(chunk)
             wait_bytes(fd, f_send, 2, chunk, crew - 1)
+        stores[6].start()
         for store in stores:
             store.wait()
 
@@ -627,7 +648,7 @@
     scratch = [
         wide, wide, wide, wide, wide, wide,
         vmem((width, TAPS), F32),
-        wide, wide, wide, wide, wide, wide,
+        wide, wide, wide, wide,
         vmem((width, TAPS), F32),
         vmem((1, width), F32),
         vmem((n, ROWS), jnp.int32),
@@ -636,8 +657,8 @@
         vmem((keys, ROWS), F32),
         vmem((TAPS, width), F32),
         vmem((2 * ROWS, width), F32),
-        wide,
-        wide,
+        vmem((2, ROWS, width // 2), BF16),
+        vmem((2, ROWS, width // 2), BF16),
         vmem((GROUP, 2 * ROWS, width), F32),
         vmem((ROWS, width), F32),
         vmem((ROWS, width), F32),
@@ -651,11 +672,15 @@
         wide,
         vmem((GROUP, 2 * ROWS - GROUP, LANES), F32),
         vmem((TAPS, width), F32),
-        vmem((chunks, crew, 2 * crew_taps, LANES), BF16),
-        vmem((chunks, crew - 1, 2 * crew_taps, LANES), BF16),
-        vmem((chunks, pairs, 2 * crew_taps, LANES), BF16),
-        vmem((chunks, crew, 2 * crew_taps, LANES), BF16),
+        vmem((chunks, crew, sides * crew_taps, LANES), BF16),
+        vmem((chunks, crew - 1, sides * crew_taps, LANES), BF16),
+        vmem((chunks, pairs, sides * crew_taps, LANES), BF16),
+        vmem((chunks, crew, sides * crew_taps, LANES), BF16),
         vmem((heads, SPAN + 1, 2, ROWS, HEAD_DIM), BF16),
+        vmem((heads, 2, ROWS, HEAD_DIM), BF16),
+        vmem((heads, 2, ROWS, HEAD_DIM), BF16),
+        vmem((heads, ROWS, HEAD_DIM), BF16),
+        vmem((heads, ROWS, HEAD_DIM), BF16),
         vmem((heads, 2, keys, HEAD_DIM), F32),
         vmem((heads, 2, 2, ROWS, HEAD_DIM), BF16),
         vmem((heads, 2, 2, ROWS, HEAD_DIM), BF16),
@@ -663,18 +688,18 @@
         vmem((heads, 2, ROWS, HEAD_DIM), BF16),
         vmem((heads, 2, ROWS, HEAD_DIM), BF16),
         vmem((heads, 2, ROWS, HEAD_DIM), BF16),
-        dma((9 + 2 * heads,)),
-        dma((2,)),
-        dma((2,)),
+        dma((7 + 4 * heads,)),
+        dma((3,)),
+        dma((3,)),
         dma((max(1, m - 1),)),
         dma((max(1, m - 1),)),
+        dma((heads, 5)),
+        dma((heads, 5)),
         dma((heads, 4)),
         dma((heads, 4)),
-        dma((heads, 3)),
-        dma((heads, 3)),
         dma((3, chunks)),
         dma((3, chunks)),
-        pltpu.SemaphoreType.REGULAR((2,)),
+        pltpu.SemaphoreType.REGULAR((3,)),
         dma((7,)),
     ]
     return kernel, scratch

time: 53.1 us -> 49.4 us (0.930)
  Pallas kernels: 52.3 us -> 48.5 us
    pallas_call x1, Pallas kernels: 50.1 us -> 46.4 us  [body(): pl.pallas_call(kernel, out_shape=shapes, in_specs=[far] * 11, out_specs=(...]
where the time goes in v3:
time: 49.4 us; the launch traced here: 49.2 us
  Pallas kernels  48.5 us (98%)
  between operations  0.64 us (1%)
    pallas_call x1, Pallas kernels, body(): pl.pallas_call(kernel, out_shape=shapes, in_specs=[far] * 11, out_specs=(...  46.4 us
    pallas_call x1, Pallas kernels, body(): pl.pallas_call(write_out, out_shape=shapes, in_specs=[far] * 7, out_specs...  2.12 us

profile of v3, /device:TPU:1, one launch (start us, length us, event | category | flops | bytes accessed | tf_op | source)
XLA Modules:
  0.0 49.2 jit_solution(2469977138195580328)
XLA Ops:
  0.6 46.4 %shard_map.162 = (bf16[128,512]{1,0:T(8,128)(2,1)}, bf16[128,512]{1,0:T(8,128)(2,1)}, bf16[128,512]{1,0:T(8,128)(2,1)}, bf16[128,512]{1,0:T(8,128)(2,1)}, bf16[1...) custom-call(bf16[128,512]{1,0:T(8,128)(2,1)} %aq_in.1, bf16[128,512]{1,0:T(8,128)(2,1)} %ak_in.1, ...), custom_call_target="tpu_custom_call" | custom-call | tf_op jit(solution)/shard_map/pallas_call | solution.py:737
  47.1 2.1 %shard_map.163 = (bf16[128,512]{1,0:T(8,128)(2,1)}, bf16[128,512]{1,0:T(8,128)(2,1)}, bf16[128,512]{1,0:T(8,128)(2,1)}, bf16[128,512]{1,0:T(8,128)(2,1)}, bf16[1...) custom-call(bf16[128,512]{1,0:T(8,128)(2,1)} %get-tuple-element.14.refs_0_, ...), custom_call_target="tpu_custom_call" | custom-call | tf_op jit(solution)/shard_map/pallas_call | solution.py:747

commit v4 on v3

--- a/solution.py
+++ b/solution.py
@@ -61,7 +61,7 @@
     def kernel(
         aq_in, ak_in, av_in, ao_in, hq_in, hk_in, hv_in, ho_in, taps_in, gain_in, seg_in,
         daq_out, dak_out, dav_out, dhq_out, dhk_out, dhv_out, dfilter_out,
-        daq, dak, dav, dhq, dhk, dhv, dfilter,
+        daq, dak, dav, dhq, dhk, dhv,
         hq, hk, hv, ho, taps, gain, seg,
         segrows, segcols, bias, taps_t, ext, halo_out, halo_in, shifts,
         mixed, gated, weighted, squares, crossed, sums, sums_in,
@@ -150,7 +150,7 @@
             pltpu.make_async_copy(src, dst, store_sem.at[place])
             for place, (src, dst) in enumerate((
                 (daq, daq_out), (dak, dak_out), (dav, dav_out), (dhq, dhq_out), (dhk, dhk_out),
-                (dhv, dhv_out), (dfilter, dfilter_out),
+                (dhv, dhv_out), (fd, dfilter_out),
             ))
         ]
 
@@ -457,38 +457,36 @@
         sig_copy = copy(sig_out, sig_in, one_send.at[2], one_recv.at[2], {"ctx": before})
         sig_copy.start()
         stores[3].start()
-        def correlate(column):
-            part = lanes(column)
-            own = segcols[ROWS : 2 * ROWS, :]
-            signal = sig[:ROWS, part]
+        def correlate(quad):
             row = lax.broadcasted_iota(jnp.int32, (GROUP, LANES), 0)
-
-            @pl.loop(0, quads)
-            def _(quad):
-                span = PART + GROUP * (QUAD - 1)
+            span = PART + GROUP * (QUAD - 1)
+
+            @pl.loop(0, columns)
+            def _(column):
+                part = lanes(column)
                 for piece in range(pieces):
                     rows = slice(piece * PART, (piece + 1) * PART)
-                    first = pl.multiple_of(
-                        ROWS + piece * PART - GROUP * (QUAD * quad + QUAD - 1), GROUP
-                    )
-                    segs = segcols[pl.ds(first, span), :]
+                    own = segcols[ROWS + piece * PART : ROWS + (piece + 1) * PART, :]
+                    signal = sig[rows, part]
+                    first = ROWS + piece * PART - GROUP * (QUAD * quad + QUAD - 1)
+                    segs = segcols[first : first + span, :]
                     masked = [
-                        jnp.where(segs[off : off + PART] == own[rows], signal[rows], 0.0)
+                        jnp.where(segs[off : off + PART] == own, signal, 0.0)
                         for off in range(GROUP * (QUAD - 1), -1, -GROUP)
                     ]
                     found = [[] for _ in range(QUAD)]
                     for r in range(GROUP):
-                        block = shifts[r, pl.ds(first, span), part]
+                        block = shifts[r, first : first + span, part]
                         for k in range(QUAD):
                             off = GROUP * (QUAD - 1 - k)
                             term = masked[k] * block[off : off + PART]
                             found[k].append(term.reshape(PART // 8, 8, LANES).sum(axis=0))
                     for k in range(QUAD):
-                        begin = pl.multiple_of(GROUP * (QUAD * quad + k), GROUP)
+                        begin = GROUP * (QUAD * quad + k)
                         total = fold(found[k], row)
                         if piece:
-                            total = total + ft[pl.ds(begin, GROUP), part]
-                        ft[pl.ds(begin, GROUP), part] = total
+                            total = total + ft[begin : begin + GROUP, part]
+                        ft[begin : begin + GROUP, part] = total
 
         def fa_copy(chunk, step):
             other, device = crew_peer(step)
@@ -514,17 +512,17 @@
             ref = held.at[chunk, pl.ds(0, count)]
             pltpu.make_async_copy(ref, ref, sems.at[phase, chunk]).wait()
 
-        def start_all(make, chunk, count):
-            @pl.loop(1, count)
-            def _(step):
-                make(chunk, step).start()
-
-        def filter_out(chunk):
-            for owner in range(crew):
+        def filter_out(quad):
+            owned = GROUP * QUAD // crew_taps
+            for owner in range(quad * owned, (quad + 1) * owned):
                 rows = slice(owner * crew_taps, (owner + 1) * crew_taps)
-                tile = [ft[rows, lanes(sides * chunk + side)] for side in range(sides)]
-                fa_out[chunk, owner] = jnp.concatenate(tile).astype(BF16)
-            start_all(fa_copy, chunk, crew)
+                tile = [ft[rows, lanes(side)] for side in range(sides)]
+                fa_out[0, owner] = jnp.concatenate(tile).astype(BF16)
+                step = lax.rem(owner - member + crew, crew)
+
+                @pl.when(step != 0)
+                def _():
+                    fa_copy(0, step).start()
 
         def filter_sum(chunk):
             wait_bytes(fa_in, f_recv, 0, chunk, crew - 1)
@@ -543,15 +541,11 @@
             for place in range(1, pairs):
                 total = total + fb[chunk, place].astype(F32)
             fd[chunk, member] = (total * (n * ROWS) ** (-0.5)).astype(BF16)
-            start_all(fd_copy, chunk, crew)
+            for step in sorted(range(1, crew), key=lambda step: -min(step, crew - step)):
+                fd_copy(chunk, step).start()
 
         def filter_done(chunk):
             wait_bytes(fd, f_recv, 2, chunk, crew - 1)
-            for side in range(sides):
-                rows = slice(side * crew_taps, (side + 1) * crew_taps)
-                taps_row = fd[chunk, :, rows].astype(F32).reshape(TAPS, LANES)
-                begin = (sides * chunk + side) * LANES
-                dfilter[begin : begin + LANES, :] = taps_row.T
 
         def spread(column):
             part = lanes(column)
@@ -588,14 +582,17 @@
                 dhv[rows, part] = (found * hk[rows, part].astype(F32)).astype(BF16)
 
         correlate(0)
+        hear(2)
+        filter_out(0)
         give_grads(0)
         service(1)
         correlate(1)
+        filter_out(1)
         service(2)
         correlate(2)
+        filter_out(2)
         correlate(3)
-        hear(2)
-        filter_out(0)
+        filter_out(3)
         attend(1)
         service(3)
         attend(2)
@@ -603,10 +600,10 @@
         attend(3)
         filter_sum(0)
         give_grads(2)
+        give_grads(3)
         sig_copy.wait_recv()
         sig[ROWS:, :] = sig_in[...].astype(F32)
         spread(0)
-        give_grads(3)
         spread(1)
         spread(2)
         spread(3)
@@ -636,8 +633,9 @@
             wait_bytes(fb, f_send, 1, chunk, pairs - 1)
         for chunk in range(chunks):
             filter_done(chunk)
+        stores[6].start()
+        for chunk in range(chunks):
             wait_bytes(fd, f_send, 2, chunk, crew - 1)
-        stores[6].start()
         for store in stores:
             store.wait()
 
@@ -647,7 +645,6 @@
     wide = vmem((ROWS, width), BF16)
     scratch = [
         wide, wide, wide, wide, wide, wide,
-        vmem((width, TAPS), F32),
         wide, wide, wide, wide,
         vmem((width, TAPS), F32),
         vmem((1, width), F32),
@@ -702,23 +699,33 @@
         pltpu.SemaphoreType.REGULAR((3,)),
         dma((7,)),
     ]
-    return kernel, scratch
+    return kernel, scratch, (chunks, crew, sides * crew_taps, LANES)
 
 
 def write_out(*refs):
-    count = (len(refs) - 1) // 3
-    sources, results, held, sems = refs[:count], refs[count : 2 * count], refs[2 * count : -1], refs[-1]
+    sources, results, held, (dfilter, sems) = refs[:7], refs[7:14], refs[14:21], refs[21:]
     loads = [
         pltpu.make_async_copy(src, mid, sems.at[0, place])
         for place, (src, mid) in enumerate(zip(sources, held))
     ]
     stores = [
         pltpu.make_async_copy(mid, dst, sems.at[1, place])
-        for place, (mid, dst) in enumerate(zip(held, results))
+        for place, (mid, dst) in enumerate(zip((*held[:6], dfilter), results))
     ]
-    for load in loads:
+    for load in reversed(loads):
         load.start()
-    for load, store in zip(loads, stores):
+    loads[6].wait()
+    fd = held[6]
+    chunks, crew, rows, _ = fd.shape
+    taps = TAPS // crew
+    sides = rows // taps
+    for chunk in range(chunks):
+        for side in range(sides):
+            tap_rows = fd[chunk, :, side * taps : (side + 1) * taps].astype(F32)
+            begin = (sides * chunk + side) * LANES
+            dfilter[begin : begin + LANES, :] = tap_rows.reshape(TAPS, LANES).T
+    stores[6].start()
+    for load, store in zip(loads[:6], stores[:6]):
         load.wait()
         store.start()
     for store in stores:
@@ -730,13 +737,14 @@
 
     def body(aq, ak, av, ao, hq, hk, hv, ho, taps, gain, seg):
         rows, width = aq.shape
-        kernel, scratch = make_kernel(n, m, width, line)
+        kernel, scratch, rows_shape = make_kernel(n, m, width, line)
         wide = jax.ShapeDtypeStruct((rows, width), BF16)
         shapes = (wide,) * 6 + (jax.ShapeDtypeStruct((width, TAPS), F32),)
+        found_shapes = (wide,) * 6 + (jax.ShapeDtypeStruct(rows_shape, BF16),)
         far = pl.BlockSpec(memory_space=pltpu.HBM)
         found = pl.pallas_call(
             kernel,
-            out_shape=shapes,
+            out_shape=found_shapes,
             in_specs=[far] * 11,
             out_specs=(far,) * 7,
             scratch_shapes=scratch,
@@ -749,8 +757,8 @@
             out_shape=shapes,
             in_specs=[far] * 7,
             out_specs=(far,) * 7,
-            scratch_shapes=[pltpu.VMEM(one.shape, one.dtype) for one in shapes]
-            + [pltpu.SemaphoreType.DMA((2, 7))],
+            scratch_shapes=[pltpu.VMEM(one.shape, one.dtype) for one in found_shapes]
+            + [pltpu.VMEM((width, TAPS), F32), pltpu.SemaphoreType.DMA((2, 7))],
             compiler_params=pltpu.CompilerParams(vmem_limit_bytes=60 * 2**20),
         )(*found)
 

time: 49.4 us -> 48.9 us (0.990)
    pallas_call x1, Pallas kernels: 46.4 us -> 45.9 us  [body(): pl.pallas_call(kernel, out_shape=found_shapes, in_specs=[far] * 11, out_s...]
where the time goes in v4:
time: 48.9 us; the launch traced here: 48.7 us
  Pallas kernels  48.1 us (98%)
  between operations  0.64 us (1%)
    pallas_call x1, Pallas kernels, body(): pl.pallas_call(kernel, out_shape=found_shapes, in_specs=[far] * 11, out_s...  45.9 us
    pallas_call x1, Pallas kernels, body(): pl.pallas_call(write_out, out_shape=shapes, in_specs=[far] * 7, out_specs...  2.24 us

profile of v4, /device:TPU:1, one launch (start us, length us, event | category | flops | bytes accessed | tf_op | source)
XLA Modules:
  0.0 48.7 jit_solution(12837071978462064617)
XLA Ops:
  0.6 45.9 %shard_map.162 = (bf16[128,512]{1,0:T(8,128)(2,1)}, bf16[128,512]{1,0:T(8,128)(2,1)}, bf16[128,512]{1,0:T(8,128)(2,1)}, bf16[128,512]{1,0:T(8,128)(2,1)}, bf16[1...) custom-call(bf16[128,512]{1,0:T(8,128)(2,1)} %aq_in.1, bf16[128,512]{1,0:T(8,128)(2,1)} %ak_in.1, ...), custom_call_target="tpu_custom_call" | custom-call | tf_op jit(solution)/shard_map/pallas_call | solution.py:745
  46.5 2.2 %shard_map.163 = (bf16[128,512]{1,0:T(8,128)(2,1)}, bf16[128,512]{1,0:T(8,128)(2,1)}, bf16[128,512]{1,0:T(8,128)(2,1)}, bf16[128,512]{1,0:T(8,128)(2,1)}, bf16[1...) custom-call(bf16[128,512]{1,0:T(8,128)(2,1)} %get-tuple-element.14.refs_0_, ...), custom_call_target="tpu_custom_call" | custom-call | tf_op jit(solution)/shard_map/pallas_call | solution.py:755

commit v5 on v4

--- a/solution.py
+++ b/solution.py
@@ -249,11 +249,10 @@
             bias[back_by * ROWS : (back_by + 1) * ROWS, :] = jnp.where(allowed, 0.0, FAR)
 
         def shift_rows(start, stop, begin, end):
-            @pl.loop(begin, end)
-            def _(column):
-                part = lanes(column)
-                for r in range(GROUP):
-                    same = segcols[start - r : stop - r, :] == segcols[start:stop, :]
+            for r in range(GROUP):
+                same = segcols[start - r : stop - r, :] == segcols[start:stop, :]
+                for column in range(begin, end):
+                    part = slice(column * LANES, (column + 1) * LANES)
                     shifts[r, start:stop, part] = jnp.where(
                         same, ext[start - r : stop - r, part], 0.0
                     )
@@ -449,14 +448,12 @@
         def _(column):
             part = lanes(column)
             slope = squares[...] * weighted[:, part] - gated[:, part] * crossed[...]
-            dhq[:, part] = (slope * mixed[:, part]).astype(BF16)
             signal = slope * hq[:, part].astype(F32)
             sig[:ROWS, part] = signal
             sig_out[:, part] = signal.astype(BF16)
 
         sig_copy = copy(sig_out, sig_in, one_send.at[2], one_recv.at[2], {"ctx": before})
         sig_copy.start()
-        stores[3].start()
         def correlate(quad):
             row = lax.broadcasted_iota(jnp.int32, (GROUP, LANES), 0)
             span = PART + GROUP * (QUAD - 1)
@@ -601,6 +598,14 @@
         filter_sum(0)
         give_grads(2)
         give_grads(3)
+
+        @pl.loop(0, columns)
+        def _(column):
+            part = lanes(column)
+            slope = squares[...] * weighted[:, part] - gated[:, part] * crossed[...]
+            dhq[:, part] = (slope * mixed[:, part]).astype(BF16)
+
+        stores[3].start()
         sig_copy.wait_recv()
         sig[ROWS:, :] = sig_in[...].astype(F32)
         spread(0)

time: 48.9 us -> 48.9 us (level)
  no operation moved by 1% of the time
where the time goes in v5:
time: 48.9 us; the launch traced here: 48.7 us
  Pallas kernels  48.1 us (98%)
  between operations  0.64 us (1%)
    pallas_call x1, Pallas kernels, body(): pl.pallas_call(kernel, out_shape=found_shapes, in_specs=[far] * 11, out_s...  45.8 us
    pallas_call x1, Pallas kernels, body(): pl.pallas_call(write_out, out_shape=shapes, in_specs=[far] * 7, out_specs...  2.24 us

profile of v5, /device:TPU:1, one launch (start us, length us, event | category | flops | bytes accessed | tf_op | source)
XLA Modules:
  0.0 48.7 jit_solution(1400882147171148266)
XLA Ops:
  0.6 45.8 %shard_map.162 = (bf16[128,512]{1,0:T(8,128)(2,1)}, bf16[128,512]{1,0:T(8,128)(2,1)}, bf16[128,512]{1,0:T(8,128)(2,1)}, bf16[128,512]{1,0:T(8,128)(2,1)}, bf16[1...) custom-call(bf16[128,512]{1,0:T(8,128)(2,1)} %aq_in.1, bf16[128,512]{1,0:T(8,128)(2,1)} %ak_in.1, ...), custom_call_target="tpu_custom_call" | custom-call | tf_op jit(solution)/shard_map/pallas_call | solution.py:750
  46.5 2.2 %shard_map.163 = (bf16[128,512]{1,0:T(8,128)(2,1)}, bf16[128,512]{1,0:T(8,128)(2,1)}, bf16[128,512]{1,0:T(8,128)(2,1)}, bf16[128,512]{1,0:T(8,128)(2,1)}, bf16[1...) custom-call(bf16[128,512]{1,0:T(8,128)(2,1)} %get-tuple-element.14.refs_0_, ...), custom_call_target="tpu_custom_call" | custom-call | tf_op jit(solution)/shard_map/pallas_call | solution.py:760
